TPU v7x, 256 devices: a whole 4x4x8 slice. The times are simulated.
256 devices in a mesh: lat: 8 (over x, y_lo), lon: 32 (over z, y_hi, core).
Axes of the slice: x: 4, y: 4 (y_hi: 2, y_lo: 2; y = y_hi * 2 + y_lo), z: 8, core: 2. Of those that a mesh axis runs over, the one named last changes fastest.
Arguments:
- inputs: bfloat16 [128, 4096, 64], P('lat', 'lon'), may hold values from -6 to 6
- pre_first: bfloat16 [128, 4096, 128], P('lat', 'lon'), may hold values from -6 to 6
- grad_out: bfloat16 [64, 2048, 128], P('lat', 'lon'), may hold values from -6 to 6
- w_first: bfloat16 [3, 3, 64, 128], replicated, may hold values from -0.25 to 0.25
- w_second: bfloat16 [3, 3, 128, 128], replicated, may hold values from -0.1875 to 0.1875
Outputs:
- grad_inputs: bfloat16 [128, 4096, 64], P('lat', 'lon')
- grad_w_first: float32 [3, 3, 64, 128], replicated
- grad_w_second: float32 [3, 3, 128, 128], replicated
All inputs are finite; a program needn't handle non-finite values.
Results may differ from a plain program's by a relative error of at most 0.0049.
Values may be sent and summed in bfloat16 or wider, within the bound.
A program may use at most 64 MiB of HBM per device.

v0:
```python
import jax
import jax.numpy as jnp
from jax import lax
from jax.sharding import PartitionSpec as P

inv_root = 0.7071067811865476
density = 0.3989422804014327


def passed_along(shard, axis, by):
    peers = lax.axis_size(axis)
    return lax.ppermute(shard, axis, [(i, (i + by) % peers) for i in range(peers)])


def extended(block, sides, width):
    for axis, dim in sides:
        count = lax.axis_size(axis)
        forward = [(i, i + 1) for i in range(count - 1)]
        forward.append((count - 1, 0))
        backward = [(target, source) for source, target in forward]
        low = lax.ppermute(
            lax.slice_in_dim(block, block.shape[dim] - width, None, axis=dim), axis, forward
        )
        high = lax.ppermute(lax.slice_in_dim(block, 0, width, axis=dim), axis, backward)
        block = jnp.concatenate([low, block, high], axis=dim)
    return block


def across_values(row):
    return passed_along(row, "lon", lax.axis_size("lon") // 2)


def across_grads(row):
    return passed_along(row, "lon", lax.axis_size("lon") // 2)


def pad_values(fields):
    band = lax.axis_index("lat")
    padded = extended(fields, (("lat", 0), ("lon", 1)), 1)
    opposite = across_values(padded[1])
    top = jnp.where(band == 0, opposite, padded[0])
    bottom = jnp.where(band == lax.axis_size("lat") - 1, jnp.zeros_like(padded[-1]), padded[-1])
    return jnp.concatenate([top[None], padded[1:-1], bottom[None]], 0)


def fold_grads(grid):
    band = lax.axis_index("lat")
    first = band == 0
    final = band == lax.axis_size("lat") - 1
    opposite = across_grads(grid[0])
    row_one = grid[1] + jnp.where(first, opposite, jnp.zeros_like(opposite))
    top = jnp.where(first, jnp.zeros_like(grid[0]), grid[0])
    bottom = jnp.where(final, jnp.zeros_like(grid[-1]), grid[-1])
    grid = jnp.concatenate([top[None], row_one[None], grid[2:-1], bottom[None]], 0)
    wide = extended(grid, (("lat", 0), ("lon", 1)), 1)
    inner = wide[2:-2]
    inner = inner.at[0].add(wide[0]).at[-1].add(wide[-1])
    core = inner[:, 2:-2]
    core = core.at[:, 0].add(inner[:, 0]).at[:, -1].add(inner[:, -1])
    return core


def taps_product(padded, grads):
    rows, cols = (grads.shape[0], grads.shape[1])
    flat = grads.reshape(rows * cols, grads.shape[2])
    result = []
    for a in range(3):
        line = []
        for b in range(3):
            piece = padded[a : a + rows, b : b + cols].reshape(rows * cols, padded.shape[2])
            line.append(
                lax.dot_general(
                    piece, flat, (((0,), (0,)), ((), ())), preferred_element_type=jnp.float32
                )
            )
        result.append(jnp.stack(line, 0))
    return jnp.stack(result, 0)


def spread(grads, weight):
    rows, cols, cout = grads.shape
    cin = weight.shape[2]
    every = jnp.transpose(weight, (3, 0, 1, 2)).reshape(cout, 9 * cin)
    terms = jnp.dot(grads.reshape(rows * cols, cout), every, preferred_element_type=jnp.float32)
    terms = terms.reshape(rows, cols, 3, 3, cin)
    grid = jnp.zeros((rows + 2, cols + 2, cin), jnp.float32)
    for a in range(3):
        for b in range(3):
            grid = grid.at[a : a + rows, b : b + cols].add(terms[:, :, a, b])
    return grid


def body(inputs, pre_first, grad_out, w_first, w_second):
    first_ch = inputs.shape[2]
    value = pre_first.astype(jnp.float32)
    cdf = 0.5 * (1.0 + lax.erf(value * inv_root))
    activated = (value * cdf).astype(jnp.bfloat16)
    slope = cdf + value * jnp.exp(-0.5 * value * value) * density
    padded = pad_values(jnp.concatenate([inputs, activated], 2))
    padded_in = padded[:, :, :first_ch]
    padded_act = padded[:, :, first_ch:]
    grad_pool = jnp.repeat(jnp.repeat(grad_out, 2, 0), 2, 1) * jnp.asarray(0.25, grad_out.dtype)
    local_second = taps_product(padded_act, grad_pool)
    grad_act = fold_grads(spread(grad_pool, w_second))
    grad_pre = (grad_act * slope).astype(jnp.bfloat16)
    local_first = taps_product(padded_in, grad_pre)
    grad_inputs = fold_grads(spread(grad_pre, w_first)).astype(jnp.bfloat16)
    grad_w_first, grad_w_second = lax.psum((local_first, local_second), ("lat", "lon"))
    return (grad_inputs, grad_w_first, grad_w_second)


def solution(mesh):
    in_specs = (P("lat", "lon", None), P("lat", "lon", None), P("lat", "lon", None), P(), P())
    out_specs = (P("lat", "lon", None), P(), P())
    return jax.shard_map(body, mesh=mesh, in_specs=in_specs, out_specs=out_specs, check_vma=False)
```

profile of v0, /device:TPU:1, one launch (start us, length us, event | category | flops | bytes accessed | tf_op | source)
XLA Modules:
  0.0 447.3 jit_solution(18419216473036246453)
XLA Ops:
  7.2 1.0 broadcast_multiply_fusion
  8.7 1.4 fusion.71
  10.9 1.1 fusion.104
  12.2 1.6 fusion.17
  14.6 3.4 scatter-add.89
  18.0 3.4 add_select_fusion
  21.3 3.5 scatter-add.90
  24.8 1.4 fusion.16
  26.2 1.3 fusion.14
  27.6 2.1 scatter-add.94
  29.7 1.3 fusion.13
  31.1 2.1 scatter-add.95
  33.2 1.4 fusion.12
  34.6 1.4 fusion.10
  36.0 2.1 scatter-add.99
  38.1 1.4 fusion.9
  39.5 2.1 scatter-add.100
  41.6 2.2 collective-permute-start
  43.8 3.9 collective-permute-done
  47.7 7.1 %collective-permute-start.1 = (f32[130,128]{1,0:T(8,128)S(1)}, f32[130,128]{1,0:T(8,128)S(1)}, u32[]{:S(2)}, u32[]{:S(2)}) collective-permute-start(f32[130,128]{1,0:T(8,128)S(1)} %get-tuple-element.325), channel_id=1, source_target_pairs={{0,16},{1,17},{2,18},{3,19},{4,20},{5,21},{6,22},{7,23},{8,24},{9,... | collective-permute-start | bytes 199688 | tf_op jit(solution)/shard_map/ppermute | solution.py:12
  54.8 1.4 collective-permute-start.2
  56.7 1.5 collective-permute-done.2
  58.3 5.8 %collective-permute-start.3 = (f32[20,1,128]{2,1,0:T(1,128)S(1)}, f32[20,1,128]{2,1,0:T(1,128)S(1)}, u32[]{:S(2)}, u32[]{:S(2)}) collective-permute-start(f32[20,1,128]{2,1,0:T(1,128)S(1)} %get-tuple-element.321), channel_id=1, source_target_pairs={{0,1},{1,2},{2,3},{3,4},{4,5},{5,6},{6,7},{7,8},{8,9},{9,10},{10,1... | collective-permute-start | bytes 30728 | tf_op jit(solution)/shard_map/ppermute | solution.py:21
  65.0 3.8 collective-permute-done.4
  71.1 1.6 fusion.8
  73.5 3.0 fusion.69
  76.5 1.1 slice_bitcast_fusion.17
  77.6 3.3 fusion.68
  81.3 3.6 collective-permute-start.11
  84.8 6.0 %scatter-add.110 = f32[18,130,64]{1,2,0:T(8,128)S(1)} dynamic-update-slice(f32[18,130,64]{1,2,0:T(8,128)S(1)} %scatter-add.109, f32[16,128,64]{1,2,0:T(8,128)} %fusion.68, s32[]{:T(128)} %bitcast.10, s32[]{:T(128)} %bitcast.11, s32[]{:T(128)} %constant.655.clone.1) | dynamic-update-slice | bytes 1048580 | tf_op jit(solution)/shard_map/scatter-add | solution.py:89
  90.8 4.0 add_select_fusion.1
  94.8 6.0 %scatter-add.111 = f32[18,130,64]{1,2,0:T(8,128)S(1)} dynamic-update-slice(f32[18,130,64]{1,2,0:T(8,128)S(1)} %scatter-add.110, f32[16,128,64]{1,2,0:T(8,128)} %add_select_fusion.1, s32[]{:T(128)} %bitcast.13, s32[]{:T(128)} %bitcast.14, s32[]{:T(128)} %constant.655.clone.1) | dynamic-update-slice | bytes 1048580 | tf_op jit(solution)/shard_map/scatter-add | solution.py:89
  100.9 1.2 fusion.67
  102.1 2.0 fusion.65
  104.1 4.7 %scatter-add.115 = f32[18,130,64]{1,2,0:T(8,128)S(1)} dynamic-update-slice(f32[18,130,64]{1,2,0:T(8,128)S(1)} %fusion.67, f32[16,128,64]{1,2,0:T(8,128)} %fusion.65, s32[]{:T(128)} %constant.660.clone.1, s32[]{:T(128)} %constant.660.clone.1, s32[]{:T(128)} %constant.655.clone.1) | dynamic-update-slice | bytes 1048580 | tf_op jit(solution)/shard_map/scatter-add | solution.py:89
  108.8 2.0 fusion.64
  110.8 4.7 %scatter-add.116 = f32[18,130,64]{1,2,0:T(8,128)S(1)} dynamic-update-slice(f32[18,130,64]{1,2,0:T(8,128)S(1)} %scatter-add.115, f32[16,128,64]{1,2,0:T(8,128)} %fusion.64, s32[]{:T(128)} %constant.660.clone.1, s32[]{:T(128)} %constant.656.clone.1, s32[]{:T(128)} %constant.655.clone.1) | dynamic-update-slice | bytes 1048580 | tf_op jit(solution)/shard_map/scatter-add | solution.py:89
  115.5 1.2 fusion.63
  116.7 2.0 fusion.61
  118.7 4.7 %scatter-add.120 = f32[18,130,64]{1,2,0:T(8,128)S(1)} dynamic-update-slice(f32[18,130,64]{1,2,0:T(8,128)S(1)} %fusion.63, f32[16,128,64]{1,2,0:T(8,128)} %fusion.61, s32[]{:T(128)} %constant.656.clone.1, s32[]{:T(128)} %constant.660.clone.1, s32[]{:T(128)} %constant.655.clone.1) | dynamic-update-slice | bytes 1048580 | tf_op jit(solution)/shard_map/scatter-add | solution.py:89
  123.4 2.0 fusion.60
  125.4 4.7 %scatter-add.121 = f32[18,130,64]{1,2,0:T(8,128)S(1)} dynamic-update-slice(f32[18,130,64]{1,2,0:T(8,128)S(1)} %scatter-add.120, f32[16,128,64]{1,2,0:T(8,128)} %fusion.60, s32[]{:T(128)} %constant.656.clone.1, s32[]{:T(128)} %constant.656.clone.1, s32[]{:T(128)} %constant.655.clone.1) | dynamic-update-slice | bytes 1048580 | tf_op jit(solution)/shard_map/scatter-add | solution.py:89
  130.2 1.4 convolution_bitcast_fusion.4
  131.6 4.6 %collective-permute-done.5 = f32[1,130,64]{1,2,0:T(8,128)S(1)} collective-permute-done((f32[1,130,64]{1,2,0:T(8,128)S(1)}, f32[1,130,64]{1,2,0:T(8,128)S(1)}, u32[]{:S(2)}, u32[]{:S(2)}) %collective-permute-start.5) | collective-permute-done | bytes 33312 | tf_op jit(solution)/shard_map/ppermute | solution.py:21
  136.3 1.1 collective-permute-start.12
  137.4 4.8 %collective-permute-start.6 = (f32[130,64]{0,1:T(8,128)S(1)}, f32[130,64]{0,1:T(8,128)S(1)}, u32[]{:S(2)}, u32[]{:S(2)}) collective-permute-start(f32[130,64]{0,1:T(8,128)S(1)} %get-tuple-element.330), channel_id=1, source_target_pairs={{0,16},{1,17},{2,18},{3,19},{4,20},{5,21},{6,22},{7,23},{8,24},{9,... | collective-permute-start | bytes 99848 | tf_op jit(solution)/shard_map/ppermute | solution.py:12
  143.2 0.9 copy-done.3
  145.0 1.2 convolution_bitcast_fusion.2
  146.2 1.3 convolution_bitcast_fusion.1
  150.1 0.9 convolution_bitcast_fusion.10
  151.0 5.4 %collective-permute-start.14 = (bf16[130,192]{1,0:T(8,128)(2,1)}, bf16[130,192]{1,0:T(8,128)(2,1)}, u32[]{:S(2)}, u32[]{:S(2)}) collective-permute-start(bf16[130,192]{1,0:T(8,128)(2,1)} %get-tuple-element.326), channel_id=1, source_target_pairs={{0,16},{1,17},{2,18},{3,19},{4,20},{5,21},{6,22},{7,23},{8,24},{9,... | collective-permute-start | bytes 149768 | tf_op jit(solution)/shard_map/ppermute | solution.py:12
  157.7 0.9 convolution_bitcast_fusion.14
  158.7 1.0 convolution_bitcast_fusion.13
  160.5 1.3 fusion.103
  162.1 2.0 copy.59
  165.8 1.8 copy.60
  167.6 1.7 collective-permute-done.9
  169.3 1.8 copy.61
  171.2 1.9 pad_maximum_fusion.1
  173.1 1.0 copy-done.13
  183.4 1.9 scatter-add.129
  186.1 250.8 %all-reduce.5.cloned.1.call-done = (f32[3,3,64,128]{3,2,1,0:T(8,128)}, f32[3,3,128,128]{3,2,1,0:T(8,128)}) async-done(((f32[3,3,64,128]{3,2,1,0:T(8,128)}, f32[3,3,128,128]{3,2,1,0:T(8,128)}), (f32[3,3,64,128]{3,2,1,0:T(8,128)}, f32[3,3,128,128]{3,2,1,0:T(8,128)})) %all-reduce.5.cloned.1.call-update) | async-done | bytes 884752 | tf_op jit(solution)/shard_map/psum | solution.py:108
  436.9 1.7 copy.151
  438.6 1.9 copy.152
  (146 shorter events, 25.4 us)
Async XLA Ops:
  7.2 1.5 copy-start
  7.2 429.7 %all-reduce.5.cloned.1.call-start = ((), (), s32[]{:S(2)}) async-start(), calls=%async_computation | async-start | bytes 1769472 | tf_op jit(solution)/shard_map/psum | solution.py:108
  8.7 1.4 copy-start.10
  10.1 3.7 copy-start.1
  12.2 1.7 copy-start.30
  41.6 6.1 %collective-permute-start = (f32[1,130,128]{2,1,0:T(8,128)S(1)}, f32[1,130,128]{2,1,0:T(8,128)S(1)}, u32[]{:S(2)}, u32[]{:S(2)}) collective-permute-start(f32[1,130,128]{2,1,0:T(8,128)S(1)} %slice_select_fusion), channel_id=1, source_target_pairs={{0,32},{32,64},{64,96},{96,128},{128,160},{160,192},{192,224},{224... | collective-permute-start | bytes 199688 | tf_op jit(solution)/shard_map/ppermute | solution.py:21
  47.7 8.9 %collective-permute-start.1 = (f32[130,128]{1,0:T(8,128)S(1)}, f32[130,128]{1,0:T(8,128)S(1)}, u32[]{:S(2)}, u32[]{:S(2)}) collective-permute-start(f32[130,128]{1,0:T(8,128)S(1)} %get-tuple-element.325), channel_id=1, source_target_pairs={{0,16},{1,17},{2,18},{3,19},{4,20},{5,21},{6,22},{7,23},{8,24},{9,... | collective-permute-start | bytes 199688 | tf_op jit(solution)/shard_map/ppermute | solution.py:12
  54.8 3.5 collective-permute-start.2
  56.6 7.5 %copy-start.18 = (bf16[16,128,64]{1,2,0:T(8,128)(2,1)S(1)}, bf16[16,128,64]{1,2,0:T(8,128)(2,1)}, u32[]{:S(2)}) copy-start(bf16[16,128,64]{1,2,0:T(8,128)(2,1)} %param.57) | copy-start | bytes 786436
  58.3 6.6 %collective-permute-start.3 = (f32[20,1,128]{2,1,0:T(1,128)S(1)}, f32[20,1,128]{2,1,0:T(1,128)S(1)}, u32[]{:S(2)}, u32[]{:S(2)}) collective-permute-start(f32[20,1,128]{2,1,0:T(1,128)S(1)} %get-tuple-element.321), channel_id=1, source_target_pairs={{0,1},{1,2},{2,3},{3,4},{4,5},{5,6},{6,7},{7,8},{8,9},{9,10},{10,1... | collective-permute-start | bytes 30728 | tf_op jit(solution)/shard_map/ppermute | solution.py:21
  64.1 4.6 %collective-permute-start.4 = (f32[20,1,128]{2,1,0:T(1,128)S(1)}, f32[20,1,128]{2,1,0:T(1,128)S(1)}, u32[]{:S(2)}, u32[]{:S(2)}) collective-permute-start(f32[20,1,128]{2,1,0:T(1,128)S(1)} %get-tuple-element.322), channel_id=1, source_target_pairs={{1,0},{2,1},{3,2},{4,3},{5,4},{6,5},{7,6},{8,7},{9,8},{10,9},{11,1... | collective-permute-start | bytes 30728 | tf_op jit(solution)/shard_map/ppermute | solution.py:24
  64.4 77.8 %copy-start.7 = (bf16[16,128,64]{2,1,0:T(8,128)(2,1)}, bf16[16,128,64]{2,1,0:T(8,128)(2,1)S(1)}, u32[]{:S(2)}) copy-start(bf16[16,128,64]{2,1,0:T(8,128)(2,1)S(1)} %copy.62) | copy-start | bytes 786436
  69.0 1.0 copy-start.17
  71.0 2.5 copy-start.24
  72.7 69.5 %copy-start.2 = (bf16[16,128,128]{2,1,0:T(8,128)(2,1)}, bf16[16,128,128]{2,1,0:T(8,128)(2,1)S(1)}, u32[]{:S(2)}) copy-start(bf16[16,128,128]{2,1,0:T(8,128)(2,1)S(1)} %get-tuple-element.333) | copy-start | bytes 1572868
  81.2 55.0 %collective-permute-start.10 = (bf16[1,128,192]{2,1,0:T(8,128)(2,1)S(1)}, bf16[1,128,192]{2,1,0:T(8,128)(2,1)S(1)}, u32[]{:S(2)}, u32[]{:S(2)}) collective-permute-start(bf16[1,128,192]{2,1,0:T(8,128)(2,1)S(1)} %get-tuple-element.331), channel_id=1, source_target_pairs={{0,32},{32,64},{64,96},{96,128},{128,160},{160,192},{192,224},{224... | collective-permute-start | bytes 147464 | tf_op jit(solution)/shard_map/ppermute | solution.py:21
  81.3 54.9 %collective-permute-start.11 = (bf16[1,128,192]{2,1,0:T(8,128)(2,1)S(1)}, bf16[1,128,192]{2,1,0:T(8,128)(2,1)S(1)}, u32[]{:S(2)}, u32[]{:S(2)}) collective-permute-start(bf16[1,128,192]{2,1,0:T(8,128)(2,1)S(1)} %get-tuple-element.332), channel_id=1, source_target_pairs={{32,0},{64,32},{96,64},{128,96},{160,128},{192,160},{224,192},{0,2... | collective-permute-start | bytes 147464 | tf_op jit(solution)/shard_map/ppermute | solution.py:24
  130.1 6.0 %collective-permute-start.5 = (f32[1,130,64]{1,2,0:T(8,128)S(1)}, f32[1,130,64]{1,2,0:T(8,128)S(1)}, u32[]{:S(2)}, u32[]{:S(2)}) collective-permute-start(f32[1,130,64]{1,2,0:T(8,128)S(1)} %slice_select_fusion.1), channel_id=1, source_target_pairs={{0,32},{32,64},{64,96},{96,128},{128,160},{160,192},{192,224},{224... | collective-permute-start | bytes 99848 | tf_op jit(solution)/shard_map/ppermute | solution.py:21
  136.3 5.9 %collective-permute-start.12 = (bf16[18,1,192]{2,1,0:T(2,128)(2,1)S(1)}, bf16[18,1,192]{2,1,0:T(2,128)(2,1)S(1)}, u32[]{:S(2)}, u32[]{:S(2)}) collective-permute-start(bf16[18,1,192]{2,1,0:T(2,128)(2,1)S(1)} %get-tuple-element.328), channel_id=1, source_target_pairs={{0,1},{1,2},{2,3},{3,4},{4,5},{5,6},{6,7},{7,8},{8,9},{9,10},{10,1... | collective-permute-start | bytes 20744 | tf_op jit(solution)/shard_map/ppermute | solution.py:21
  137.4 4.8 %collective-permute-start.13 = (bf16[18,1,192]{2,1,0:T(2,128)(2,1)S(1)}, bf16[18,1,192]{2,1,0:T(2,128)(2,1)S(1)}, u32[]{:S(2)}, u32[]{:S(2)}) collective-permute-start(bf16[18,1,192]{2,1,0:T(2,128)(2,1)S(1)} %get-tuple-element.329), channel_id=1, source_target_pairs={{1,0},{2,1},{3,2},{4,3},{5,4},{6,5},{7,6},{8,7},{9,8},{10,9},{11,1... | collective-permute-start | bytes 20744 | tf_op jit(solution)/shard_map/ppermute | solution.py:24
  137.4 22.9 %collective-permute-start.6 = (f32[130,64]{0,1:T(8,128)S(1)}, f32[130,64]{0,1:T(8,128)S(1)}, u32[]{:S(2)}, u32[]{:S(2)}) collective-permute-start(f32[130,64]{0,1:T(8,128)S(1)} %get-tuple-element.330), channel_id=1, source_target_pairs={{0,16},{1,17},{2,18},{3,19},{4,20},{5,21},{6,22},{7,23},{8,24},{9,... | collective-permute-start | bytes 99848 | tf_op jit(solution)/shard_map/ppermute | solution.py:12
  142.2 18.2 %collective-permute-start.7 = (f32[1,130,64]{1,2,0:T(8,128)S(1)}, f32[1,130,64]{1,2,0:T(8,128)S(1)}, u32[]{:S(2)}, u32[]{:S(2)}) collective-permute-start(f32[1,130,64]{1,2,0:T(8,128)S(1)} %get-tuple-element.318), channel_id=1, source_target_pairs={{32,0},{64,32},{96,64},{128,96},{160,128},{192,160},{224,192},{0,2... | collective-permute-start | bytes 99848 | tf_op jit(solution)/shard_map/ppermute | solution.py:24
  142.2 15.5 %copy-start.20 = (bf16[18,1,192]{2,1,0:T(2,128)(2,1)}, bf16[18,1,192]{2,1,0:T(2,128)(2,1)S(1)}, u32[]{:S(2)}) copy-start(bf16[18,1,192]{2,1,0:T(2,128)(2,1)S(1)} %collective-permute-done.12) | copy-start | bytes 20740
  142.2 16.4 %copy-start.22 = (bf16[18,1,192]{2,1,0:T(2,128)(2,1)}, bf16[18,1,192]{2,1,0:T(2,128)(2,1)S(1)}, u32[]{:S(2)}) copy-start(bf16[18,1,192]{2,1,0:T(2,128)(2,1)S(1)} %collective-permute-done.13) | copy-start | bytes 20740
  143.1 1.0 copy-start.3
  143.1 1.2 copy-start.8
  143.1 1.9 copy-start.11
  151.0 23.8 %collective-permute-start.14 = (bf16[130,192]{1,0:T(8,128)(2,1)}, bf16[130,192]{1,0:T(8,128)(2,1)}, u32[]{:S(2)}, u32[]{:S(2)}) collective-permute-start(bf16[130,192]{1,0:T(8,128)(2,1)} %get-tuple-element.326), channel_id=1, source_target_pairs={{0,16},{1,17},{2,18},{3,19},{4,20},{5,21},{6,22},{7,23},{8,24},{9,... | collective-permute-start | bytes 149768 | tf_op jit(solution)/shard_map/ppermute | solution.py:12
  160.5 1.3 copy-start.5
  162.0 9.2 %copy-start.6 = (f32[20,130,64]{1,2,0:T(8,128)S(1)}, f32[20,130,64]{1,2,0:T(8,128)}, u32[]{:S(2)}) copy-start(f32[20,130,64]{1,2,0:T(8,128)} %copy-done.5) | copy-start | bytes 1996804
  162.0 3.8 collective-permute-start.8
  164.1 5.2 %collective-permute-start.9 = (f32[20,1,64]{2,1,0:T(1,128)}, f32[20,1,64]{2,1,0:T(1,128)}, u32[]{:S(2)}, u32[]{:S(2)}) collective-permute-start(f32[20,1,64]{2,1,0:T(1,128)} %copy.59), channel_id=1, source_target_pairs={{1,0},{2,1},{3,2},{4,3},{5,4},{6,5},{7,6},{8,7},{9,8},{10,9},{11,1... | collective-permute-start | bytes 15368 | tf_op jit(solution)/shard_map/ppermute | solution.py:24
  173.0 1.1 copy-start.13
  173.0 1.3 copy-start.14
  174.4 1.0 copy-start.4
  174.4 1.6 copy-start.9
  174.5 1.6 copy-start.21
  174.5 1.6 copy-start.23
  174.6 3.0 copy-start.15
  174.6 2.4 copy-start.12
  179.5 0.8 copy-start.28
  179.5 0.9 copy-start.29
  179.6 1.0 copy-start.19
  180.4 1.0 copy-start.25
  180.4 1.0 copy-start.26
  180.4 1.0 copy-start.27
  180.5 1.7 copy-start.16
Sparse Core Ops, SparseCore 0:
  182.3 254.5 all-reduce.4
where the time goes:
time: 449 us; the launch traced here: 447 us
  waiting for transfers between devices  267 us (59%)
  local copies, waits for them, and re-layouts  69.3 us (15%)
  other arithmetic  44.8 us (10%)
  starting transfers between devices  32.6 us (7%)
  matrix products  18.6 us (4%)
  between operations  14.9 us (3%)
    psum x1, waiting for transfers between devices, body(): lax.psum((local_first, local_second), ('lat', 'lon'))  251 us
    scatter-add x14, local copies, waits for them, and re-layouts, spread(): grid = grid.at[a:a + rows, b:b + cols].add(terms[:, :, a, b])  46.2 us
    add x10, other arithmetic, spread(): grid = grid.at[a:a + rows, b:b + cols].add(terms[:, :, a, b])  18.6 us
    ppermute x3, starting transfers between devices, passed_along(): lax.ppermute(shard, axis, [(i, (i + by) % peers) for i in range(peers)])  17.3 us
    dot_general x18, matrix products, taps_product(): lax.dot_general(piece, flat, (((0,), (0,)), ((), ())), preferred_element_...  14.2 us
    ppermute x6, starting transfers between devices, extended(): lax.ppermute(lax.slice_in_dim(block, block.shape[dim] - width, None, axis...  9.36 us
    unnamed x69, local copies, waits for them, and re-layouts  9.2 us
  transfers between devices with their start and end apart: 16, of which 8 were waited for; matrix products, arithmetic and copies ran while one was open for 16% of the time, Pallas kernels for 0%

commit v1 on v0

v1 whole, which is shorter than its diff:
```python
import functools

import jax
import jax.numpy as jnp
from jax import lax
from jax.experimental import pallas as pl
from jax.experimental.pallas import tpu as pltpu
from jax.sharding import PartitionSpec as P

INV_ROOT = 0.7071067811865476
DENSITY = 0.3989422804014327
BF16 = jnp.bfloat16
F32 = jnp.float32
MESH = pl.DeviceIdType.MESH

ROWS, COLS, C0, C1 = 16, 128, 64, 128
WIDE = COLS + 32
PWIDE = COLS // 2 + 16
GROUPS = 4


def gelu_parts(value):
    cdf = 0.5 * (1.0 + lax.erf(value * INV_ROOT))
    act = value * cdf
    slope = cdf + value * jnp.exp(-0.5 * value * value) * DENSITY
    return act, slope


def dot(a, b):
    return lax.dot_general(a, b, (((1,), (0,)), ((), ())), preferred_element_type=F32)


def kernel(
    nlat, nlon,
    pre_h, in_h, go_h, w1_h, w2_h,
    gi_o, gw_o,
    pre_v, in_v, go_v, w1_v, w2_v, wa, wb,
    e_s, row_s, e_r, row_r, hc, hs, hg,
    act_f, slope_f, act3, pext, gpt, in3, g_v, ga_f, gi_v,
    acc, p1s, p1r, p2s, p2r, zb, res,
    load_sem, halo_send, halo_recv, p1_send, p1_recv, p2_send, p2_recv,
    z_send, z_recv, p4_send, p4_recv, p5_send, p5_recv, out_sem,
):
    lat, lon = lax.axis_index("lat"), lax.axis_index("lon")
    nq, nz = nlat * 2, nlon // 4
    chunk = 1024 // nq
    per = nq // GROUPS
    z, yhi, core = lon // 4, (lon % 4) // 2, lon % 2
    q = lat * 2 + yhi
    is_pole = lat == 0
    is_last = lat == nlat - 1
    half = nlon // 2

    def chip(p, k):
        return (p // 2, z * 4 + (p % 2) * 2 + k)

    def at(dlat, dlon):
        return (dlat, lax.rem(dlon + 2 * nlon, nlon))

    loads = [
        pltpu.make_async_copy(src, dst, load_sem.at[i])
        for i, (src, dst) in enumerate(
            ((pre_h, pre_v), (in_h, in_v), (go_h, go_v), (w2_h, w2_v), (w1_h, w1_v))
        )
    ]
    for load in loads:
        load.start()

    barrier = pltpu.get_barrier_semaphore()

    def greet(device):
        pl.semaphore_signal(barrier, inc=1, device_id=device, device_id_type=MESH)

    top_lat = jnp.where(is_pole, 0, lat - 1)
    top_lon = jnp.where(is_pole, lon + half, lon)
    for d in (-1, 1):
        greet(at(lat, lon + d))
    for d in (-1, 0, 1):
        greet(at(top_lat, top_lon + d))

    @pl.when(jnp.logical_not(is_last))
    def _():
        for d in (-1, 0, 1):
            greet(at(lat + 1, lon + d))

    greet(chip(q, 1 - core))
    for k in range(1, nq):
        greet(chip(lax.rem(q + k, nq), core))
    for k in range(1, nz):
        greet((lat, lax.rem(lon + 4 * k, nlon)))

    loads[0].wait()
    loads[1].wait()
    loads[2].wait()
    lane = lax.broadcasted_iota(jnp.int32, (C0, 128), 1)
    sub = lax.broadcasted_iota(jnp.int32, (16, 128), 0)
    zero16 = jnp.zeros((16, 128), F32)
    for side, (col, first) in enumerate(((0, 0), (15, 112))):
        edge = zero16
        for r in range(ROWS):
            tile = pre_v[r, first : first + 16, :].astype(F32)
            edge = jnp.where(sub == r, jnp.broadcast_to(tile[col : col + 1], (16, 128)), edge)
        e_s[side, 0:16, :] = edge.astype(BF16)
        edge = zero16
        for r in range(ROWS // 2):
            tile = go_v[r, first // 112 * 48 : first // 112 * 48 + 16, :].astype(F32)
            edge = jnp.where(sub == r, jnp.broadcast_to(tile[col : col + 1], (16, 128)), edge)
        e_s[side, 16:32, :] = edge.astype(BF16)
        edge = jnp.zeros((C0, 128), F32)
        for r in range(ROWS):
            shift = r if side == 0 else r + 1
            edge = jnp.where(lane == r, pltpu.roll(in_v[r].astype(F32), shift, 1), edge)
        e_s[side, 32:96, :] = edge.astype(BF16)
    for end, r in enumerate((0, ROWS - 1)):
        row_s[end, 0:128, :] = pre_v[r]
        row_s[end, 128:192, :] = in_v[r]
        row_s[end, 192:256, :] = go_v[r // 2]

    pl.semaphore_wait(barrier, jnp.where(is_last, 0, 3) + 2 + 3 + 1 + (nq - 1) + (nz - 1))

    up = jnp.where(is_pole, 0, 2)
    up_row = jnp.where(is_pole, 0, 1)

    def edge_copy(number, side, slot, device):
        return pltpu.make_async_remote_copy(
            src_ref=e_s.at[side], dst_ref=e_r.at[slot], send_sem=halo_send.at[number],
            recv_sem=halo_recv.at[slot], device_id=device, device_id_type=MESH,
        )

    def row_copy(number, end, slot, device):
        return pltpu.make_async_remote_copy(
            src_ref=row_s.at[end], dst_ref=row_r.at[slot], send_sem=halo_send.at[number],
            recv_sem=halo_recv.at[6 + slot], device_id=device, device_id_type=MESH,
        )

    always = [
        row_copy(0, 0, up_row, at(top_lat, top_lon)),
        edge_copy(1, 1, 1, at(lat, lon + 1)),
        edge_copy(2, 0, 4, at(lat, lon - 1)),
        edge_copy(3, 1, up, at(top_lat, top_lon + 1)),
        edge_copy(4, 0, up + 3, at(top_lat, top_lon - 1)),
    ]
    down = [
        row_copy(5, 1, 0, at(lat + 1, lon)),
        edge_copy(6, 1, 0, at(lat + 1, lon + 1)),
        edge_copy(7, 0, 3, at(lat + 1, lon - 1)),
    ]
    for copy in always:
        copy.start()

    @pl.when(jnp.logical_not(is_last))
    def _():
        for copy in down:
            copy.start()

    @pl.when(is_last)
    def _():
        e_r[2] = jnp.zeros((96, 128), BF16)
        e_r[5] = jnp.zeros((96, 128), BF16)
        row_r[1] = jnp.zeros((256, 128), BF16)

    loads[3].wait()
    loads[4].wait()
    for a in range(3):
        for b in range(3):
            t = w2_v[3 * a + b].astype(F32).T.astype(BF16)
            wa[0, 128 * a : 128 * a + 128, 128 * b : 128 * b + 128] = t
            u = w1_v[3 * a + b].astype(F32).T.astype(BF16)
            wb[0, 128 * a : 128 * a + 128, 64 * b : 64 * b + 64] = u
    wa[1] = wa[0]
    wb[1] = wb[0]

    @pl.when(is_pole)
    def _():
        wa[1, 256:384, :] = wa[0, 0:128, :]
        wb[1, 256:384, :] = wb[0, 0:128, :]

    @pl.loop(0, ROWS)
    def _(r):
        act, slope = gelu_parts(pre_v[r].astype(F32))
        act_f[r + 1, 0:128, :] = act
        slope_f[r + 1, 0:128, :] = slope

    copies = lax.broadcasted_iota(jnp.int32, (64, 128), 1) // 2
    copies = jnp.where(copies == lax.broadcasted_iota(jnp.int32, (64, 128), 0), 0.25, 0.0).astype(BF16)
    gpt[:, 0:256] = jnp.zeros((128, 256), BF16)
    gpt[:, 18 * 128 : 20 * 128] = jnp.zeros((128, 256), BF16)
    for i in range(ROWS // 2):
        t = lax.dot_general(
            go_v[i], copies, (((0,), (0,)), ((), ())), preferred_element_type=F32
        ).astype(BF16)
        gpt[:, (2 * i + 2) * 128 : (2 * i + 3) * 128] = t
        gpt[:, (2 * i + 3) * 128 : (2 * i + 4) * 128] = t

    for number in range(5):
        always[number].wait_send()

    @pl.when(jnp.logical_not(is_last))
    def _():
        for copy in down:
            copy.wait_send()

    def arrived(slot):
        dst = e_r.at[slot] if slot < 6 else row_r.at[slot - 6]
        pltpu.make_async_copy(dst, dst, halo_recv.at[slot]).wait()

    for slot in (1, 4, 0, 3, 6):
        arrived(slot)

    @pl.when(jnp.logical_not(is_last))
    def _():
        for slot in (2, 5, 7):
            arrived(slot)

    keep = jnp.where(is_last, 0.0, 1.0).astype(F32)
    for side in range(2):
        top = e_r[3 * side, 0:32, :].astype(F32)
        mid = e_r[3 * side + 1, 0:32, :].astype(F32)
        low = e_r[3 * side + 2, 0:32, :].astype(F32)
        hc[side, 0:8, :] = jnp.broadcast_to(jnp.where(is_pole, top[0:1], top[15:16]), (8, 128))
        hc[side, 8:24, :] = mid[0:16]
        hc[side, 24:32, :] = jnp.broadcast_to(low[0:1], (8, 128))
        act, slope = gelu_parts(hc[side])
        hc[side] = act
        hs[side] = slope
        hg[side, 0:8, :] = 0.25 * jnp.broadcast_to(jnp.where(is_pole, top[16:17], top[23:24]), (8, 128))
        hg[side, 8:16, :] = 0.25 * mid[16:24]
        hg[side, 16:24, :] = 0.25 * jnp.broadcast_to(low[16:17], (8, 128))
    for end, t in enumerate((0, 17)):
        act, slope = gelu_parts(row_r[end, 0:128, :].astype(F32))
        act_f[t, 0:128, :] = act
        slope_f[t, 0:128, :] = slope if end == 0 else slope * keep
    for t in range(18):
        scale = keep if t == 17 else 1.0
        for side, place in enumerate((152, 128)):
            act_f[t, place : place + 8, :] = jnp.broadcast_to(hc[side, t + 7 : t + 8, :], (8, 128))
            slope_f[t, place : place + 8, :] = scale * jnp.broadcast_to(hs[side, t + 7 : t + 8, :], (8, 128))

    for i in range(10):
        part = go_v[i - 1] if 0 < i < 9 else row_r[0 if i == 0 else 1, 192:256, :]
        pext[i, 0:64, :] = (0.25 * part.astype(F32)).astype(BF16)
        left = jnp.broadcast_to(hg[0, i + 7 : i + 8, :], (16, 128))
        right = jnp.broadcast_to(hg[1, i + 7 : i + 8, :], (16, 128))
        tile = jnp.where(sub == 0, right, jnp.where(sub == 15, left, 0.0))
        pext[i, 64:80, :] = tile.astype(BF16)

    @pl.loop(0, 18)
    def _(t):
        x = act_f[t]
        rows = pl.ds(pl.multiple_of(t * 128, 128), 128)
        act3[rows, 0:128] = pltpu.roll(x, 1, 0)[0:128].astype(BF16)
        act3[rows, 128:256] = x[0:128].astype(BF16)
        act3[rows, 256:384] = pltpu.roll(x, WIDE - 1, 0)[0:128].astype(BF16)

    lhs = jnp.concatenate([gpt[:, (2 - a) * 128 : (2 - a) * 128 + 18 * 128] for a in range(3)], 0)
    both = dot(lhs, act3[...])
    for a in range(3):
        for b in range(3):
            block = both[128 * a : 128 * a + 128, 128 * b : 128 * b + 128]
            acc[(3 * a + b) * 128 : (3 * a + b + 1) * 128, :] = block.T

    @pl.loop(0, 9)
    def _(i):
        here, after = pext[i], pext[i + 1]
        lhs = jnp.concatenate(
            [jnp.concatenate([after, here, here], 1), jnp.concatenate([after, after, here], 1)], 0
        )
        taps = wa[jnp.where(i == 0, 1, 0)]
        terms = dot(lhs, taps)
        for s in range(2):
            part = terms[PWIDE * s : PWIDE * (s + 1)]
            t0, t1, t2 = part[:, 0:128], part[:, 128:256], part[:, 256:384]
            ga_f[s, pl.ds(0, PWIDE, stride=2), :] = t0 + t1 + pltpu.roll(t2, 1, 0)
            ga_f[s, pl.ds(1, PWIDE, stride=2), :] = pltpu.roll(t0, PWIDE - 1, 0) + t1 + t2
            g_v[2 * i + s] = (ga_f[s] * slope_f[2 * i + s]).astype(BF16)

    for t in range(18):
        if 0 < t < 17:
            x = in_v[t - 1].astype(F32)
            left = pltpu.roll(e_r[1, 32:96, :].astype(F32), (129 - t) % 128, 1)
            right = pltpu.roll(e_r[4, 32:96, :].astype(F32), 128 - t, 1)
        elif t == 0:
            x = row_r[0, 128:192, :].astype(F32)
            left = e_r[0, 32:96, :].astype(F32)
            left = jnp.where(is_pole, left, pltpu.roll(left, 128 - 15, 1))
            right = e_r[3, 32:96, :].astype(F32)
            right = jnp.where(is_pole, pltpu.roll(right, 127, 1), pltpu.roll(right, 112, 1))
        else:
            x = row_r[1, 128:192, :].astype(F32)
            left = e_r[2, 32:96, :].astype(F32)
            right = pltpu.roll(e_r[5, 32:96, :].astype(F32), 127, 1)
        cells = slice(128 * t, 128 * t + 128)
        in3[0:64, cells] = jnp.where(lane == 0, left, pltpu.roll(x, 1, 1)).astype(BF16)
        in3[64:128, cells] = x.astype(BF16)
        in3[128:192, cells] = jnp.where(lane == 127, right, pltpu.roll(x, 127, 1)).astype(BF16)

    lhs = jnp.concatenate([in3[:, a * 128 : a * 128 + 2048] for a in range(3)], 0)
    acc[1152:1728, :] = dot(lhs, g_v[1:17, 0:128, :].reshape(2048, 128))
    acc[1728:2048, :] = jnp.zeros((320, 128), F32)

    p1s[...] = acc[pl.ds(pl.multiple_of((1 - core) * 1024, 1024), 1024), :].astype(BF16)

    def group(i):
        return lax.rem(q // per + i, GROUPS)

    def group_rows(g):
        return pl.ds(pl.multiple_of(g * (per * chunk), 64), per * chunk)

    def p1_copy(i):
        rows = group_rows(group(i))
        return pltpu.make_async_remote_copy(
            src_ref=p1s.at[rows], dst_ref=p1r.at[rows], send_sem=p1_send.at[i], recv_sem=p1_recv.at[i],
            device_id=chip(q, 1 - core), device_id_type=MESH,
        )

    order = (1, 2, 3, 0)
    for i in order:
        p1_copy(i).start()

    def p2_copy(p):
        rows = pl.ds(pl.multiple_of(p * chunk, 64), chunk)
        return pltpu.make_async_remote_copy(
            src_ref=p2s.at[rows], dst_ref=p2r.at[q], send_sem=p2_send.at[p], recv_sem=p2_recv.at[q],
            device_id=chip(p, core), device_id_type=MESH,
        )

    for i in order:
        p1_copy(i).wait()
        rows = group_rows(group(i))
        own = pl.ds(pl.multiple_of(core * 1024 + group(i) * (per * chunk), 64), per * chunk)
        total = acc[own, :] + p1r[rows, :].astype(F32)
        acc[own, :] = total
        p2s[rows, :] = total.astype(BF16)
        for j in range(per):
            p = group(i) * per + lax.rem(q + j, per)
            if i == 0 and j == 0:
                continue
            p2_copy(p).start()

    @pl.loop(0, ROWS)
    def _(r):
        lhs = jnp.concatenate([g_v[r + 2], g_v[r + 1], g_v[r]], 1)
        terms = dot(lhs, wb[jnp.where(r == 0, 1, 0)])
        t01, t2 = terms[:, 0:128], terms[:, 128:192]
        first = lax.broadcasted_iota(jnp.int32, (128, 128), 1) < 64
        t01 = jnp.where(first, pltpu.roll(t01, WIDE - 1, 0)[0:128], t01[0:128]).T
        t2 = pltpu.roll(t2, 1, 0)[0:128].T
        gi_v[r] = (t01[0:64] + t01[64:128] + t2).astype(BF16)

    gi_copy = pltpu.make_async_copy(gi_v, gi_o, out_sem.at[0])
    gi_copy.start()

    total = acc[pl.ds(pl.multiple_of(core * 1024 + q * chunk, 64), chunk), :]
    for k in range(1, nq):
        p = lax.rem(q + nq - k, nq)
        pltpu.make_async_copy(p2r.at[p], p2r.at[p], p2_recv.at[p]).wait()
        total = total + p2r[p].astype(F32)
    zb[z] = total.astype(BF16)

    def z_copy(k):
        return pltpu.make_async_remote_copy(
            src_ref=zb.at[z], dst_ref=zb.at[z], send_sem=z_send.at[k], recv_sem=z_recv.at[z],
            device_id=(lat, lax.rem(lon + 4 * k, nlon)), device_id_type=MESH,
        )

    for k in range(1, nz):
        z_copy(k).start()
    for k in range(1, nz):
        p = lax.rem(z + nz - k, nz)
        pltpu.make_async_copy(zb.at[p], zb.at[p], z_recv.at[p]).wait()
    total = zb[0].astype(F32)
    for k in range(1, nz):
        total = total + zb[k].astype(F32)
    mine = pl.ds(pl.multiple_of(q * chunk, 64), chunk)
    res[core, mine, :] = total.astype(BF16)

    def p4_copy(p):
        return pltpu.make_async_remote_copy(
            src_ref=res.at[core, mine], dst_ref=res.at[core, mine], send_sem=p4_send.at[p],
            recv_sem=p4_recv.at[q], device_id=chip(p, core), device_id_type=MESH,
        )

    for k in range(1, nq):
        p4_copy(lax.rem(q + k, nq)).start()

    def p5_copy(i):
        rows = group_rows(group(i))
        return pltpu.make_async_remote_copy(
            src_ref=res.at[core, rows], dst_ref=res.at[core, rows], send_sem=p5_send.at[i],
            recv_sem=p5_recv.at[i], device_id=chip(q, 1 - core), device_id_type=MESH,
        )

    for i in (0, 3, 2, 1):
        for j in range(per):
            p = group(i) * per + lax.rem(q + per - j, per)
            if i == 0 and j == 0:
                continue
            there = pl.ds(pl.multiple_of(p * chunk, 64), chunk)
            pltpu.make_async_copy(res.at[core, there], res.at[core, there], p4_recv.at[p]).wait()
        p5_copy(i).start()
    for i in (0, 3, 2, 1):
        rows = group_rows(group(i))
        other = res.at[1 - core, rows]
        pltpu.make_async_copy(other, other, p5_recv.at[i]).wait()
    outs = [pltpu.make_async_copy(res.at[k], gw_o.at[pl.ds(1024 * k, 1024)], out_sem.at[1 + k]) for k in range(2)]
    for copy in outs:
        copy.start()

    for k in range(1, nq):
        p2_copy(lax.rem(q + k, nq)).wait_send()
        p4_copy(lax.rem(q + k, nq)).wait_send()
    for k in range(1, nz):
        z_copy(k).wait_send()
    for i in range(GROUPS):
        p5_copy(i).wait_send()
    gi_copy.wait()
    for copy in outs:
        copy.wait()


def section(nlat, nlon, inputs, pre_first, grad_out, w_first, w_second):
    nq, nz = nlat * 2, nlon // 4
    chunk = 1024 // nq
    hbm = pl.BlockSpec(memory_space=pl.ANY)
    vmem = pltpu.VMEM
    dma = pltpu.SemaphoreType.DMA
    gi, gw = pl.pallas_call(
        functools.partial(kernel, nlat, nlon),
        out_shape=(
            jax.ShapeDtypeStruct((ROWS, C0, COLS), BF16),
            jax.ShapeDtypeStruct((2048, 128), BF16),
        ),
        in_specs=[hbm] * 5,
        out_specs=(hbm, hbm),
        scratch_shapes=[
            vmem((ROWS, COLS, C1), BF16),
            vmem((ROWS, C0, COLS), BF16),
            vmem((ROWS // 2, COLS // 2, C1), BF16),
            vmem((9, C0, C1), BF16),
            vmem((9, C1, C1), BF16),
            vmem((2, 384, 384), BF16),
            vmem((2, 384, 192), BF16),
            vmem((2, 96, 128), BF16),
            vmem((2, 256, 128), BF16),
            vmem((6, 96, 128), BF16),
            vmem((2, 256, 128), BF16),
            vmem((2, 32, 128), F32),
            vmem((2, 32, 128), F32),
            vmem((2, 24, 128), F32),
            vmem((18, WIDE, 128), F32),
            vmem((18, WIDE, 128), F32),
            vmem((18 * 128, 384), BF16),
            vmem((10, PWIDE, 128), BF16),
            vmem((128, 20 * 128), BF16),
            vmem((192, 18 * 128), BF16),
            vmem((18, WIDE, 128), BF16),
            vmem((2, WIDE, 128), F32),
            vmem((ROWS, C0, COLS), BF16),
            vmem((2048, 128), F32),
            vmem((1024, 128), BF16),
            vmem((1024, 128), BF16),
            vmem((1024, 128), BF16),
            vmem((nq, chunk, 128), BF16),
            vmem((nz, chunk, 128), BF16),
            vmem((2, 1024, 128), BF16),
            dma((5,)),
            dma((8,)), dma((8,)),
            dma((GROUPS,)), dma((GROUPS,)),
            dma((nq,)), dma((nq,)),
            dma((nz,)), dma((nz,)),
            dma((nq,)), dma((nq,)),
            dma((GROUPS,)), dma((GROUPS,)),
            dma((3,)),
        ],
        compiler_params=pltpu.CompilerParams(
            collective_id=0, has_side_effects=True, vmem_limit_bytes=40 * 1024 * 1024
        ),
        cost_estimate=pl.CostEstimate(flops=1_800_000_000, bytes_accessed=3_000_000, transcendentals=600_000),
    )(
        pre_first,
        jnp.transpose(inputs, (0, 2, 1)),
        grad_out,
        w_first.reshape(9, C0, C1),
        w_second.reshape(9, C1, C1),
    )
    grad_w_second = gw[0:1152].astype(F32).reshape(3, 3, C1, C1)
    grad_w_first = gw[1152:1728].astype(F32).reshape(3, 3, C0, C1)
    return jnp.transpose(gi, (0, 2, 1)), grad_w_first, grad_w_second


def solution(mesh):
    nlat, nlon = mesh.shape["lat"], mesh.shape["lon"]
    in_specs = (P("lat", "lon", None), P("lat", "lon", None), P("lat", "lon", None), P(), P())
    out_specs = (P("lat", "lon", None), P(), P())
    return jax.shard_map(
        functools.partial(section, nlat, nlon), mesh=mesh, in_specs=in_specs, out_specs=out_specs, check_vma=False
    )
```

time: 449 us -> 53.2 us (0.12)
  waiting for transfers between devices: 267 us -> 0 us
  local copies, waits for them, and re-layouts: 69.3 us -> 5.49 us
  Pallas kernels: 0 us -> 45.2 us
  other arithmetic: 44.8 us -> 1.6 us
  starting transfers between devices: 32.6 us -> 0 us
  matrix products: 18.6 us -> 0 us
  between operations: 14.9 us -> 0.67 us
    psum x1 -> x0, waiting for transfers between devices: 251 us -> none  [body(): lax.psum((local_first, local_second), ('lat', 'lon'))]
    scatter-add x18 -> x0, local copies, waits for them, and re-layouts: 48.8 us -> none  [the longest x14 46.2 us: spread(): grid = grid.at[a:a + rows, b:b + cols].add(terms[:, :, a, b])]
    pallas_call x0 -> x1, Pallas kernels: none -> 45.2 us  [section(): pl.pallas_call(functools.partial(kernel, nlat, nlon), out_shape=(jax.Shap...]
    ppermute x15 -> x0, starting transfers between devices: 32.5 us -> none  [the longest x3 17.3 us: passed_along(): lax.ppermute(shard, axis, [(i, (i + by) % peers) for i in range(peers)])]
    add x14 -> x0, other arithmetic: 20 us -> none  [the longest x10 18.6 us: spread(): grid = grid.at[a:a + rows, b:b + cols].add(terms[:, :, a, b])]
    dot_general x20 -> x0, matrix products: 18.6 us -> none  [the longest x18 14.2 us: taps_product(): lax.dot_general(piece, flat, (((0,), (0,)), ((), ())), preferred_element_...]
    ppermute x15 -> x0, waiting for transfers between devices: 16.4 us -> none  [the longest x6 8.97 us: extended(): lax.ppermute(lax.slice_in_dim(block, block.shape[dim] - width, None, axis...]
    another operation x10 -> x0, other arithmetic: 11.2 us -> none
  transfers between devices with their start and end apart: 16 -> 0, of which waited for: 8 -> 0; matrix products, arithmetic and copies ran while one was open for 16% -> 0% of each run, Pallas kernels for 0% -> 0%
where the time goes in v1:
time: 53.2 us; the launch traced here: 52.9 us
  Pallas kernels  45.2 us (85%)
  local copies, waits for them, and re-layouts  5.49 us (10%)
  other arithmetic  1.6 us (3%)
  between operations  0.67 us (1%)
    pallas_call x1, Pallas kernels, section(): pl.pallas_call(functools.partial(kernel, nlat, nlon), out_shape=(jax.Shap...  45.2 us
    unnamed x11, local copies, waits for them, and re-layouts  5.46 us

profile of v1, /device:TPU:1, one launch (start us, length us, event | category | flops | bytes accessed | tf_op | source)
XLA Modules:
  0.0 52.9 jit_solution(1064336305436170329)
XLA Ops:
  0.6 0.0 copy-start
  0.6 1.0 %copy-done = bf16[16,128,128]{2,1,0:T(8,128)(2,1)S(1)} copy-done((bf16[16,128,128]{2,1,0:T(8,128)(2,1)S(1)}, bf16[16,128,128]{2,1,0:T(8,128)(2,1)}, u32[]{:S(2)}) %copy-start) | copy-done | bytes 524312
  1.7 0.0 copy-start.1
  1.7 1.0 %copy-done.1 = bf16[3,3,128,128]{3,2,1,0:T(8,128)(2,1)S(1)} copy-done((bf16[3,3,128,128]{3,2,1,0:T(8,128)(2,1)S(1)}, bf16[3,3,128,128]{3,2,1,0:T(8,128)(2,1)}, u32[]{:S(2)}) %copy-start.1) | copy-done | bytes 294936
  2.6 0.0 copy-start.2
  2.6 0.9 %copy-done.2 = bf16[16,128,64]{1,2,0:T(8,128)(2,1)S(1)} copy-done((bf16[16,128,64]{1,2,0:T(8,128)(2,1)S(1)}, bf16[16,128,64]{1,2,0:T(8,128)(2,1)}, u32[]{:S(2)}) %copy-start.2) | copy-done | bytes 262168
  3.6 0.0 copy-start.3
  3.6 0.9 %copy-done.3 = bf16[3,3,64,128]{3,2,1,0:T(8,128)(2,1)S(1)} copy-done((bf16[3,3,64,128]{3,2,1,0:T(8,128)(2,1)S(1)}, bf16[3,3,64,128]{3,2,1,0:T(8,128)(2,1)}, u32[]{:S(2)}) %copy-start.3) | copy-done | bytes 147480
  4.5 0.0 copy-start.4
  4.5 0.9 %copy-done.4 = bf16[8,64,128]{2,1,0:T(8,128)(2,1)S(1)} copy-done((bf16[8,64,128]{2,1,0:T(8,128)(2,1)S(1)}, bf16[8,64,128]{2,1,0:T(8,128)(2,1)}, u32[]{:S(2)}) %copy-start.4) | copy-done | bytes 131096
  5.4 45.2 %shard_map.76 = (bf16[16,64,128]{2,1,0:T(8,128)(2,1)S(1)}, bf16[2048,128]{1,0:T(8,128)(2,1)S(1)}) custom-call(bf16[16,128,128]{2,1,0:T(8,128)(2,1)S(1)} %copy-done, bf16[16,64,128]{2,1,0:T(8,128)(2,1)S(1)} %bitcast.10, bf16[8,64,128]{2,1,0:T(8,128)(2,1)S(1)} %copy-done.4, bf16[9,64,128]{2,1,0:T(8,128)(2,1)S(1)} %bitcast.11, bf16[9,128,128]{2,1,0:T(8,128)(2,1)S(1)} %bitcast.9), custom_call_target="tpu_custom_call" | custom-call | flops 1800000000 | bytes 3000000 | tf_op jit(solution)/shard_map/pallas_call | solution.py:427
  50.6 0.7 %convert.2 = f32[3,3,64,128]{3,2,1,0:T(8,128)} convert(bf16[3,3,64,128]{3,2,1,0:T(8,128)(2,1)S(1)} %bitcast.13) | non-fusion elementwise | flops 73728 | bytes 442368 | tf_op jit(solution)/shard_map/reshape | solution.py:487
  51.4 0.9 %convert.3 = f32[3,3,128,128]{3,2,1,0:T(8,128)} convert(bf16[3,3,128,128]{3,2,1,0:T(8,128)(2,1)S(1)} %bitcast.12) | non-fusion elementwise | flops 147456 | bytes 884736 | tf_op jit(solution)/shard_map/reshape | solution.py:486
  52.2 0.7 %copy.9 = bf16[16,128,64]{1,2,0:T(8,128)(2,1)} copy(bf16[16,128,64]{1,2,0:T(8,128)(2,1)S(1)} %bitcast.8) | data formatting | bytes 524288
  (2 shorter events, 0.0 us)
Async XLA Ops:
  0.6 1.0 %copy-start = (bf16[16,128,128]{2,1,0:T(8,128)(2,1)S(1)}, bf16[16,128,128]{2,1,0:T(8,128)(2,1)}, u32[]{:S(2)}) copy-start(bf16[16,128,128]{2,1,0:T(8,128)(2,1)} %pre_h.1) | copy-start | bytes 1572868
  1.7 1.0 %copy-start.1 = (bf16[3,3,128,128]{3,2,1,0:T(8,128)(2,1)S(1)}, bf16[3,3,128,128]{3,2,1,0:T(8,128)(2,1)}, u32[]{:S(2)}) copy-start(bf16[3,3,128,128]{3,2,1,0:T(8,128)(2,1)} %param.9) | copy-start | bytes 884740
  2.6 0.9 %copy-start.2 = (bf16[16,128,64]{1,2,0:T(8,128)(2,1)S(1)}, bf16[16,128,64]{1,2,0:T(8,128)(2,1)}, u32[]{:S(2)}) copy-start(bf16[16,128,64]{1,2,0:T(8,128)(2,1)} %param.5) | copy-start | bytes 786436
  3.6 0.9 %copy-start.3 = (bf16[3,3,64,128]{3,2,1,0:T(8,128)(2,1)S(1)}, bf16[3,3,64,128]{3,2,1,0:T(8,128)(2,1)}, u32[]{:S(2)}) copy-start(bf16[3,3,64,128]{3,2,1,0:T(8,128)(2,1)} %param.8) | copy-start | bytes 442372
  4.5 0.9 %copy-start.4 = (bf16[8,64,128]{2,1,0:T(8,128)(2,1)S(1)}, bf16[8,64,128]{2,1,0:T(8,128)(2,1)}, u32[]{:S(2)}) copy-start(bf16[8,64,128]{2,1,0:T(8,128)(2,1)} %go_h.1) | copy-start | bytes 393220

commit v2 on v1

--- a/solution.py
+++ b/solution.py
@@ -35,11 +35,11 @@
     pre_h, in_h, go_h, w1_h, w2_h,
     gi_o, gw_o,
     pre_v, in_v, go_v, w1_v, w2_v, wa, wb,
-    e_s, row_s, e_r, row_r, hc, hs, hg,
-    act_f, slope_f, act3, pext, gpt, in3, g_v, ga_f, gi_v,
+    e_s, row_s, e_r, row_r, hc, hs, hg, hi,
+    act_f, slope_f, act3, pext, gpt, gpt_top, in3, g_v, ga_f, both,
     acc, p1s, p1r, p2s, p2r, zb, res,
     load_sem, halo_send, halo_recv, p1_send, p1_recv, p2_send, p2_recv,
-    z_send, z_recv, p4_send, p4_recv, p5_send, p5_recv, out_sem,
+    z_send, z_recv, p4_send, p4_recv, p5_send, p5_recv,
 ):
     lat, lon = lax.axis_index("lat"), lax.axis_index("lon")
     nq, nz = nlat * 2, nlon // 4
@@ -110,16 +110,16 @@
         for r in range(ROWS):
             shift = r if side == 0 else r + 1
             edge = jnp.where(lane == r, pltpu.roll(in_v[r].astype(F32), shift, 1), edge)
-        e_s[side, 32:96, :] = edge.astype(BF16)
+        e_s[side, 32:48, 0:64] = edge.T[0:16].astype(BF16)
+        e_s[side, 32:48, 64:128] = jnp.zeros((16, 64), BF16)
     for end, r in enumerate((0, ROWS - 1)):
         row_s[end, 0:128, :] = pre_v[r]
-        row_s[end, 128:192, :] = in_v[r]
-        row_s[end, 192:256, :] = go_v[r // 2]
+        row_s[end, 128:192, :] = go_v[r // 2]
+        row_s[end, 192:256, :] = in_v[r]
 
     pl.semaphore_wait(barrier, jnp.where(is_last, 0, 3) + 2 + 3 + 1 + (nq - 1) + (nz - 1))
 
     up = jnp.where(is_pole, 0, 2)
-    up_row = jnp.where(is_pole, 0, 1)
 
     def edge_copy(number, side, slot, device):
         return pltpu.make_async_remote_copy(
@@ -127,14 +127,15 @@
             recv_sem=halo_recv.at[slot], device_id=device, device_id_type=MESH,
         )
 
-    def row_copy(number, end, slot, device):
-        return pltpu.make_async_remote_copy(
-            src_ref=row_s.at[end], dst_ref=row_r.at[slot], send_sem=halo_send.at[number],
+    def row_copy(number, end, slot, device, size=256):
+        return pltpu.make_async_remote_copy(
+            src_ref=row_s.at[end, pl.ds(0, size)], dst_ref=row_r.at[slot, pl.ds(0, size)], send_sem=halo_send.at[number],
             recv_sem=halo_recv.at[6 + slot], device_id=device, device_id_type=MESH,
         )
 
+    turned = row_copy(0, 0, 0, at(0, lon + half), 192)
+    above = row_copy(0, 0, 1, at(lat - 1, lon))
     always = [
-        row_copy(0, 0, up_row, at(top_lat, top_lon)),
         edge_copy(1, 1, 1, at(lat, lon + 1)),
         edge_copy(2, 0, 4, at(lat, lon - 1)),
         edge_copy(3, 1, up, at(top_lat, top_lon + 1)),
@@ -145,6 +146,14 @@
         edge_copy(6, 1, 0, at(lat + 1, lon + 1)),
         edge_copy(7, 0, 3, at(lat + 1, lon - 1)),
     ]
+    @pl.when(is_pole)
+    def _():
+        turned.start()
+
+    @pl.when(jnp.logical_not(is_pole))
+    def _():
+        above.start()
+
     for copy in always:
         copy.start()
 
@@ -155,8 +164,8 @@
 
     @pl.when(is_last)
     def _():
-        e_r[2] = jnp.zeros((96, 128), BF16)
-        e_r[5] = jnp.zeros((96, 128), BF16)
+        e_r[2] = jnp.zeros((48, 128), BF16)
+        e_r[5] = jnp.zeros((48, 128), BF16)
         row_r[1] = jnp.zeros((256, 128), BF16)
 
     loads[3].wait()
@@ -192,19 +201,11 @@
         gpt[:, (2 * i + 2) * 128 : (2 * i + 3) * 128] = t
         gpt[:, (2 * i + 3) * 128 : (2 * i + 4) * 128] = t
 
-    for number in range(5):
-        always[number].wait_send()
-
-    @pl.when(jnp.logical_not(is_last))
-    def _():
-        for copy in down:
-            copy.wait_send()
-
     def arrived(slot):
         dst = e_r.at[slot] if slot < 6 else row_r.at[slot - 6]
         pltpu.make_async_copy(dst, dst, halo_recv.at[slot]).wait()
 
-    for slot in (1, 4, 0, 3, 6):
+    for slot in (1, 4):
         arrived(slot)
 
     @pl.when(jnp.logical_not(is_last))
@@ -213,59 +214,66 @@
             arrived(slot)
 
     keep = jnp.where(is_last, 0.0, 1.0).astype(F32)
+    zero8 = jnp.zeros((8, 128), F32)
     for side in range(2):
-        top = e_r[3 * side, 0:32, :].astype(F32)
-        mid = e_r[3 * side + 1, 0:32, :].astype(F32)
-        low = e_r[3 * side + 2, 0:32, :].astype(F32)
-        hc[side, 0:8, :] = jnp.broadcast_to(jnp.where(is_pole, top[0:1], top[15:16]), (8, 128))
+        mid = e_r[3 * side + 1].astype(F32)
+        low = e_r[3 * side + 2].astype(F32)
         hc[side, 8:24, :] = mid[0:16]
         hc[side, 24:32, :] = jnp.broadcast_to(low[0:1], (8, 128))
-        act, slope = gelu_parts(hc[side])
-        hc[side] = act
-        hs[side] = slope
-        hg[side, 0:8, :] = 0.25 * jnp.broadcast_to(jnp.where(is_pole, top[16:17], top[23:24]), (8, 128))
+        act, slope = gelu_parts(hc[side, 8:32, :])
+        hc[side, 8:32, :] = act
+        hs[side, 8:32, :] = slope
         hg[side, 8:16, :] = 0.25 * mid[16:24]
         hg[side, 16:24, :] = 0.25 * jnp.broadcast_to(low[16:17], (8, 128))
-    for end, t in enumerate((0, 17)):
-        act, slope = gelu_parts(row_r[end, 0:128, :].astype(F32))
-        act_f[t, 0:128, :] = act
-        slope_f[t, 0:128, :] = slope if end == 0 else slope * keep
-    for t in range(18):
+        hi[side, 0:8, :] = zero8
+        hi[side, 8:24, :] = mid[32:48]
+        hi[side, 24:32, :] = jnp.broadcast_to(low[32:33], (8, 128))
+    act, slope = gelu_parts(row_r[1, 0:128, :].astype(F32))
+    act_f[17, 0:128, :] = act
+    slope_f[17, 0:128, :] = slope * keep
+
+    def sides(t):
         scale = keep if t == 17 else 1.0
         for side, place in enumerate((152, 128)):
             act_f[t, place : place + 8, :] = jnp.broadcast_to(hc[side, t + 7 : t + 8, :], (8, 128))
             slope_f[t, place : place + 8, :] = scale * jnp.broadcast_to(hs[side, t + 7 : t + 8, :], (8, 128))
 
-    for i in range(10):
-        part = go_v[i - 1] if 0 < i < 9 else row_r[0 if i == 0 else 1, 192:256, :]
+    def pooled(i, part):
         pext[i, 0:64, :] = (0.25 * part.astype(F32)).astype(BF16)
         left = jnp.broadcast_to(hg[0, i + 7 : i + 8, :], (16, 128))
         right = jnp.broadcast_to(hg[1, i + 7 : i + 8, :], (16, 128))
         tile = jnp.where(sub == 0, right, jnp.where(sub == 15, left, 0.0))
         pext[i, 64:80, :] = tile.astype(BF16)
 
-    @pl.loop(0, 18)
-    def _(t):
+    def act_row(t):
         x = act_f[t]
         rows = pl.ds(pl.multiple_of(t * 128, 128), 128)
         act3[rows, 0:128] = pltpu.roll(x, 1, 0)[0:128].astype(BF16)
         act3[rows, 128:256] = x[0:128].astype(BF16)
         act3[rows, 256:384] = pltpu.roll(x, WIDE - 1, 0)[0:128].astype(BF16)
 
-    lhs = jnp.concatenate([gpt[:, (2 - a) * 128 : (2 - a) * 128 + 18 * 128] for a in range(3)], 0)
-    both = dot(lhs, act3[...])
-    for a in range(3):
+    for t in range(1, 18):
+        sides(t)
+    for i in range(1, 10):
+        pooled(i, go_v[i - 1] if i < 9 else row_r[1, 128:192, :])
+
+    @pl.loop(1, 18)
+    def _(t):
+        act_row(t)
+
+    lhs = jnp.concatenate([gpt[:, (3 - a) * 128 : (3 - a) * 128 + 17 * 128] for a in range(3)], 0)
+    terms = dot(lhs, act3[128:2304, :])
+    both[...] = terms[0:128]
+    for a in range(1, 3):
         for b in range(3):
-            block = both[128 * a : 128 * a + 128, 128 * b : 128 * b + 128]
+            block = terms[128 * a : 128 * a + 128, 128 * b : 128 * b + 128]
             acc[(3 * a + b) * 128 : (3 * a + b + 1) * 128, :] = block.T
 
-    @pl.loop(0, 9)
-    def _(i):
+    def grad_rows(i, taps):
         here, after = pext[i], pext[i + 1]
         lhs = jnp.concatenate(
             [jnp.concatenate([after, here, here], 1), jnp.concatenate([after, after, here], 1)], 0
         )
-        taps = wa[jnp.where(i == 0, 1, 0)]
         terms = dot(lhs, taps)
         for s in range(2):
             part = terms[PWIDE * s : PWIDE * (s + 1)]
@@ -274,29 +282,77 @@
             ga_f[s, pl.ds(1, PWIDE, stride=2), :] = pltpu.roll(t0, PWIDE - 1, 0) + t1 + t2
             g_v[2 * i + s] = (ga_f[s] * slope_f[2 * i + s]).astype(BF16)
 
-    for t in range(18):
-        if 0 < t < 17:
-            x = in_v[t - 1].astype(F32)
-            left = pltpu.roll(e_r[1, 32:96, :].astype(F32), (129 - t) % 128, 1)
-            right = pltpu.roll(e_r[4, 32:96, :].astype(F32), 128 - t, 1)
-        elif t == 0:
-            x = row_r[0, 128:192, :].astype(F32)
-            left = e_r[0, 32:96, :].astype(F32)
-            left = jnp.where(is_pole, left, pltpu.roll(left, 128 - 15, 1))
-            right = e_r[3, 32:96, :].astype(F32)
-            right = jnp.where(is_pole, pltpu.roll(right, 127, 1), pltpu.roll(right, 112, 1))
-        else:
-            x = row_r[1, 128:192, :].astype(F32)
-            left = e_r[2, 32:96, :].astype(F32)
-            right = pltpu.roll(e_r[5, 32:96, :].astype(F32), 127, 1)
+    @pl.loop(1, 9)
+    def _(i):
+        grad_rows(i, wa[0])
+
+    edges = [jnp.concatenate([hi[side], jnp.zeros((96, 128), F32)], 0).T[0:64] for side in range(2)]
+
+    def in_row(t, x, left, right):
         cells = slice(128 * t, 128 * t + 128)
         in3[0:64, cells] = jnp.where(lane == 0, left, pltpu.roll(x, 1, 1)).astype(BF16)
         in3[64:128, cells] = x.astype(BF16)
         in3[128:192, cells] = jnp.where(lane == 127, right, pltpu.roll(x, 127, 1)).astype(BF16)
 
-    lhs = jnp.concatenate([in3[:, a * 128 : a * 128 + 2048] for a in range(3)], 0)
-    acc[1152:1728, :] = dot(lhs, g_v[1:17, 0:128, :].reshape(2048, 128))
+    for t in range(1, 18):
+        x = (in_v[t - 1] if t < 17 else row_r[1, 192:256, :]).astype(F32)
+        in_row(t, x, pltpu.roll(edges[0], 121 - t, 1), pltpu.roll(edges[1], 120 - t, 1))
+
+    lhs = jnp.concatenate([in3[:, (a + 1) * 128 : (a + 16) * 128] for a in range(3)], 0)
+    acc[1152:1728, :] = dot(lhs, g_v[2:17, 0:128, :].reshape(1920, 128))
     acc[1728:2048, :] = jnp.zeros((320, 128), F32)
+
+    @pl.when(is_pole)
+    def _():
+        dst = row_r.at[0, pl.ds(0, 192)]
+        pltpu.make_async_copy(dst, dst, halo_recv.at[6]).wait()
+        row_r[0, 192:256, :] = jnp.zeros((64, 128), BF16)
+
+    @pl.when(jnp.logical_not(is_pole))
+    def _():
+        arrived(6)
+
+    arrived(0)
+    arrived(3)
+    for side in range(2):
+        top = e_r[3 * side].astype(F32)
+
+        def pick(first, last):
+            return jnp.broadcast_to(jnp.where(is_pole, top[first : first + 1], top[last : last + 1]), (8, 128))
+
+        act, slope = gelu_parts(pick(0, 15))
+        hc[side, 0:8, :] = act
+        hs[side, 0:8, :] = slope
+        hg[side, 0:8, :] = 0.25 * pick(16, 23)
+        hi[side, 0:8, :] = jnp.where(is_pole, 0.0, pick(32, 47))
+    act, slope = gelu_parts(row_r[0, 0:128, :].astype(F32))
+    act_f[0, 0:128, :] = act
+    slope_f[0, 0:128, :] = slope
+    sides(0)
+    pooled(0, row_r[0, 128:192, :])
+    grad_rows(0, wa[1])
+
+    act_row(0)
+    top_go = lax.dot_general(
+        row_r[0, 128:192, :], copies, (((0,), (0,)), ((), ())), preferred_element_type=F32
+    ).astype(BF16)
+    gpt_top[...] = jnp.where(is_pole, top_go.astype(F32), gpt[:, 256:384].astype(F32)).astype(BF16)
+
+    @pl.when(is_pole)
+    def _():
+        act3[0:128, :] = act3[128:256, :]
+
+    first_row = both[...] + dot(gpt_top[...], act3[0:128, :])
+    for b in range(3):
+        acc[b * 128 : (b + 1) * 128, :] = first_row[:, 128 * b : 128 * b + 128].T
+
+    x = row_r[0, 192:256, :].astype(F32)
+    edges = [jnp.concatenate([hi[side], jnp.zeros((96, 128), F32)], 0).T[0:64] for side in range(2)]
+    in_row(0, x, pltpu.roll(edges[0], 121, 1), pltpu.roll(edges[1], 120, 1))
+    here = jnp.concatenate([in3[:, 0:128], in3[:, 128:256], in3[:, 256:384]], 0)
+    fold = jnp.where(is_pole, in3[:, 128:256].astype(F32), 0.0).astype(BF16)
+    there = jnp.concatenate([fold, jnp.zeros((384, 128), BF16)], 0)
+    acc[1152:1728, :] += dot(jnp.concatenate([here, there], 1), jnp.concatenate([g_v[1, 0:128, :], g_v[0, 0:128, :]], 0))
 
     p1s[...] = acc[pl.ds(pl.multiple_of((1 - core) * 1024, 1024), 1024), :].astype(BF16)
 
@@ -345,10 +401,7 @@
         first = lax.broadcasted_iota(jnp.int32, (128, 128), 1) < 64
         t01 = jnp.where(first, pltpu.roll(t01, WIDE - 1, 0)[0:128], t01[0:128]).T
         t2 = pltpu.roll(t2, 1, 0)[0:128].T
-        gi_v[r] = (t01[0:64] + t01[64:128] + t2).astype(BF16)
-
-    gi_copy = pltpu.make_async_copy(gi_v, gi_o, out_sem.at[0])
-    gi_copy.start()
+        gi_o[r] = (t01[0:64] + t01[64:128] + t2).astype(BF16)
 
     total = acc[pl.ds(pl.multiple_of(core * 1024 + q * chunk, 64), chunk), :]
     for k in range(1, nq):
@@ -383,55 +436,80 @@
     for k in range(1, nq):
         p4_copy(lax.rem(q + k, nq)).start()
 
-    def p5_copy(i):
-        rows = group_rows(group(i))
-        return pltpu.make_async_remote_copy(
-            src_ref=res.at[core, rows], dst_ref=res.at[core, rows], send_sem=p5_send.at[i],
-            recv_sem=p5_recv.at[i], device_id=chip(q, 1 - core), device_id_type=MESH,
-        )
-
-    for i in (0, 3, 2, 1):
-        for j in range(per):
-            p = group(i) * per + lax.rem(q + per - j, per)
-            if i == 0 and j == 0:
-                continue
-            there = pl.ds(pl.multiple_of(p * chunk, 64), chunk)
-            pltpu.make_async_copy(res.at[core, there], res.at[core, there], p4_recv.at[p]).wait()
-        p5_copy(i).start()
-    for i in (0, 3, 2, 1):
-        rows = group_rows(group(i))
-        other = res.at[1 - core, rows]
-        pltpu.make_async_copy(other, other, p5_recv.at[i]).wait()
-    outs = [pltpu.make_async_copy(res.at[k], gw_o.at[pl.ds(1024 * k, 1024)], out_sem.at[1 + k]) for k in range(2)]
-    for copy in outs:
-        copy.start()
+    def p5_copy(p):
+        rows = pl.ds(pl.multiple_of(p * chunk, 64), chunk)
+        return pltpu.make_async_remote_copy(
+            src_ref=res.at[core, rows], dst_ref=res.at[core, rows], send_sem=p5_send.at[p],
+            recv_sem=p5_recv.at[p], device_id=chip(q, 1 - core), device_id_type=MESH,
+        )
+
+    def deliver(k, p):
+        rows = pl.ds(pl.multiple_of(p * chunk, 64), chunk)
+        gw_o[pl.ds(pl.multiple_of(k * 1024 + p * chunk, 64), chunk), :] = res[k, rows, :].astype(F32)
+
+    p5_copy(q).start()
+    deliver(core, q)
+    for k in range(1, nq):
+        p = lax.rem(q + nq - k, nq)
+        there = pl.ds(pl.multiple_of(p * chunk, 64), chunk)
+        pltpu.make_async_copy(res.at[core, there], res.at[core, there], p4_recv.at[p]).wait()
+        p5_copy(p).start()
+        deliver(core, p)
+    for k in range(nq):
+        p = lax.rem(q + nq - k, nq)
+        there = pl.ds(pl.multiple_of(p * chunk, 64), chunk)
+        other = res.at[1 - core, there]
+        pltpu.make_async_copy(other, other, p5_recv.at[p]).wait()
+        deliver(1 - core, p)
+
+    @pl.when(is_pole)
+    def _():
+        turned.wait_send()
+
+    @pl.when(jnp.logical_not(is_pole))
+    def _():
+        above.wait_send()
+
+    for copy in always:
+        copy.wait_send()
+
+    @pl.when(jnp.logical_not(is_last))
+    def _():
+        for copy in down:
+            copy.wait_send()
 
     for k in range(1, nq):
         p2_copy(lax.rem(q + k, nq)).wait_send()
         p4_copy(lax.rem(q + k, nq)).wait_send()
     for k in range(1, nz):
         z_copy(k).wait_send()
-    for i in range(GROUPS):
-        p5_copy(i).wait_send()
-    gi_copy.wait()
-    for copy in outs:
+    for p in range(nq):
+        p5_copy(p).wait_send()
+
+
+def write_out(gi_v, gw_v, gi_o, gw1_o, gw2_o, sem):
+    copies = [
+        pltpu.make_async_copy(gw_v.at[pl.ds(0, 1152)], gw2_o, sem.at[0]),
+        pltpu.make_async_copy(gw_v.at[pl.ds(1152, 576)], gw1_o, sem.at[1]),
+        pltpu.make_async_copy(gi_v, gi_o, sem.at[2]),
+    ]
+    for copy in copies:
+        copy.start()
+    for copy in copies:
         copy.wait()
 
 
 def section(nlat, nlon, inputs, pre_first, grad_out, w_first, w_second):
     nq, nz = nlat * 2, nlon // 4
     chunk = 1024 // nq
-    hbm = pl.BlockSpec(memory_space=pl.ANY)
+    hbm = pl.BlockSpec(memory_space=pltpu.HBM)
     vmem = pltpu.VMEM
     dma = pltpu.SemaphoreType.DMA
     gi, gw = pl.pallas_call(
         functools.partial(kernel, nlat, nlon),
-        out_shape=(
-            jax.ShapeDtypeStruct((ROWS, C0, COLS), BF16),
-            jax.ShapeDtypeStruct((2048, 128), BF16),
-        ),
+        out_shape=(vmem((ROWS, C0, COLS), BF16), vmem((2048, 128), F32)),
         in_specs=[hbm] * 5,
-        out_specs=(hbm, hbm),
+        out_specs=(pl.BlockSpec(memory_space=vmem), pl.BlockSpec(memory_space=vmem)),
         scratch_shapes=[
             vmem((ROWS, COLS, C1), BF16),
             vmem((ROWS, C0, COLS), BF16),
@@ -440,22 +518,24 @@
             vmem((9, C1, C1), BF16),
             vmem((2, 384, 384), BF16),
             vmem((2, 384, 192), BF16),
-            vmem((2, 96, 128), BF16),
+            vmem((2, 48, 128), BF16),
             vmem((2, 256, 128), BF16),
-            vmem((6, 96, 128), BF16),
+            vmem((6, 48, 128), BF16),
             vmem((2, 256, 128), BF16),
             vmem((2, 32, 128), F32),
             vmem((2, 32, 128), F32),
             vmem((2, 24, 128), F32),
+            vmem((2, 32, 128), F32),
             vmem((18, WIDE, 128), F32),
             vmem((18, WIDE, 128), F32),
             vmem((18 * 128, 384), BF16),
             vmem((10, PWIDE, 128), BF16),
             vmem((128, 20 * 128), BF16),
+            vmem((128, 128), BF16),
             vmem((192, 18 * 128), BF16),
             vmem((18, WIDE, 128), BF16),
             vmem((2, WIDE, 128), F32),
-            vmem((ROWS, C0, COLS), BF16),
+            vmem((128, 384), F32),
             vmem((2048, 128), F32),
             vmem((1024, 128), BF16),
             vmem((1024, 128), BF16),
@@ -469,23 +549,41 @@
             dma((nq,)), dma((nq,)),
             dma((nz,)), dma((nz,)),
             dma((nq,)), dma((nq,)),
-            dma((GROUPS,)), dma((GROUPS,)),
-            dma((3,)),
+            dma((nq,)), dma((nq,)),
         ],
         compiler_params=pltpu.CompilerParams(
             collective_id=0, has_side_effects=True, vmem_limit_bytes=40 * 1024 * 1024
         ),
         cost_estimate=pl.CostEstimate(flops=1_800_000_000, bytes_accessed=3_000_000, transcendentals=600_000),
     )(
-        pre_first,
-        jnp.transpose(inputs, (0, 2, 1)),
-        grad_out,
-        w_first.reshape(9, C0, C1),
-        w_second.reshape(9, C1, C1),
+        *(
+            pltpu.with_memory_space_constraint(x, pltpu.HBM)
+            for x in (
+                pre_first,
+                jnp.transpose(inputs, (0, 2, 1)),
+                grad_out,
+                w_first.reshape(9, C0, C1),
+                w_second.reshape(9, C1, C1),
+            )
+        )
     )
-    grad_w_second = gw[0:1152].astype(F32).reshape(3, 3, C1, C1)
-    grad_w_first = gw[1152:1728].astype(F32).reshape(3, 3, C0, C1)
-    return jnp.transpose(gi, (0, 2, 1)), grad_w_first, grad_w_second
+    gi, grad_w_first, grad_w_second = pl.pallas_call(
+        write_out,
+        out_shape=(
+            jax.ShapeDtypeStruct((ROWS, C0, COLS), BF16),
+            jax.ShapeDtypeStruct((9 * C0, C1), F32),
+            jax.ShapeDtypeStruct((9 * C1, C1), F32),
+        ),
+        in_specs=[pl.BlockSpec(memory_space=vmem)] * 2,
+        out_specs=(pl.BlockSpec(memory_space=pl.ANY),) * 3,
+        scratch_shapes=[dma((3,))],
+        compiler_params=pltpu.CompilerParams(vmem_limit_bytes=16 * 1024 * 1024),
+    )(gi, gw)
+    return (
+        jnp.transpose(gi, (0, 2, 1)),
+        grad_w_first.reshape(3, 3, C0, C1),
+        grad_w_second.reshape(3, 3, C1, C1),
+    )
 
 
 def solution(mesh):

time: 53.2 us -> 44.5 us (0.84)
  local copies, waits for them, and re-layouts: 5.49 us -> 0 us
  other arithmetic: 1.6 us -> 0 us
  Pallas kernels: 45.2 us -> 43.8 us
    unnamed x11 -> x0, local copies, waits for them, and re-layouts: 5.46 us -> none
    reshape x2 -> x0, other arithmetic: 1.6 us -> none  [the longest x1 0.86 us: section(): grad_w_second = gw[0:1152].astype(F32).reshape(3, 3, C1, C1)]
    pallas_call x1 -> x2, Pallas kernels: 45.2 us -> 43.8 us  [the longest x1 42.7 us: section(): pl.pallas_call(functools.partial(kernel, nlat, nlon), out_shape=(vmem((RO...]
where the time goes in v2:
time: 44.5 us; the launch traced here: 44.4 us
  Pallas kernels  43.8 us (98%)
  between operations  0.64 us (1%)
    pallas_call x1, Pallas kernels, section(): pl.pallas_call(functools.partial(kernel, nlat, nlon), out_shape=(vmem((RO...  42.7 us
    pallas_call x1, Pallas kernels, section(): pl.pallas_call(write_out, out_shape=(jax.ShapeDtypeStruct((ROWS, C0, COLS...  1.02 us

profile of v2, /device:TPU:1, one launch (start us, length us, event | category | flops | bytes accessed | tf_op | source)
XLA Modules:
  0.0 44.4 jit_solution(11081788085820365946)
XLA Ops:
  0.6 42.7 %shard_map.76 = (bf16[16,64,128]{2,1,0:T(8,128)(2,1)S(1)}, f32[2048,128]{1,0:T(8,128)S(1)}) custom-call(bf16[16,128,128]{2,1,0:T(8,128)(2,1)} %pre_h.1, bf16[16,64,128]{2,1,0:T(8,128)(2,1)} %bitcast.9, bf16[8,64,128]{2,1,0:T(8,128)(2,1)} %go_h.1, bf16[9,64,128]{2,1,0:T(8,128)(2,1)} %bitcast.11, bf16[9,128,128]{2,1,0:T(8,128)(2,1)} %bitcast.7), custom_call_target="tpu_custom_call" | custom-call | flops 1800000000 | bytes 3000000 | tf_op jit(solution)/shard_map/pallas_call | solution.py:508
  43.4 1.0 %shard_map.77 = (bf16[16,64,128]{2,1,0:T(8,128)(2,1)}, f32[576,128]{1,0:T(8,128)}, f32[1152,128]{1,0:T(8,128)}) custom-call(bf16[16,64,128]{2,1,0:T(8,128)(2,1)S(1)} %get-tuple-element.8.gi_v, f32[2048,128]{1,0:T(8,128)S(1)} %get-tuple-element.9.gw_v), custom_call_target="tpu_custom_call" | custom-call | tf_op jit(solution)/shard_map/pallas_call | solution.py:570

commit v3 on v2

--- a/solution.py
+++ b/solution.py
@@ -16,7 +16,11 @@
 ROWS, COLS, C0, C1 = 16, 128, 64, 128
 WIDE = COLS + 32
 PWIDE = COLS // 2 + 16
-GROUPS = 4
+HALF = 512
+
+
+def far_first(n):
+    return sorted(range(1, n), key=lambda k: (-min(k, n - k), k))
 
 
 def gelu_parts(value):
@@ -43,8 +47,7 @@
 ):
     lat, lon = lax.axis_index("lat"), lax.axis_index("lon")
     nq, nz = nlat * 2, nlon // 4
-    chunk = 1024 // nq
-    per = nq // GROUPS
+    chunk = HALF // nq
     z, yhi, core = lon // 4, (lon % 4) // 2, lon % 2
     q = lat * 2 + yhi
     is_pole = lat == 0
@@ -73,10 +76,14 @@
 
     top_lat = jnp.where(is_pole, 0, lat - 1)
     top_lon = jnp.where(is_pole, lon + half, lon)
+    for d in (-1, 0, 1):
+        greet(at(top_lat, top_lon + d))
+    for k in far_first(nz):
+        greet((lat, lax.rem(lon + 4 * k, nlon)))
+    for k in far_first(nq):
+        greet(chip(lax.rem(q + k, nq), core))
     for d in (-1, 1):
         greet(at(lat, lon + d))
-    for d in (-1, 0, 1):
-        greet(at(top_lat, top_lon + d))
 
     @pl.when(jnp.logical_not(is_last))
     def _():
@@ -84,10 +91,6 @@
             greet(at(lat + 1, lon + d))
 
     greet(chip(q, 1 - core))
-    for k in range(1, nq):
-        greet(chip(lax.rem(q + k, nq), core))
-    for k in range(1, nz):
-        greet((lat, lax.rem(lon + 4 * k, nlon)))
 
     loads[0].wait()
     loads[1].wait()
@@ -136,16 +139,19 @@
     turned = row_copy(0, 0, 0, at(0, lon + half), 192)
     above = row_copy(0, 0, 1, at(lat - 1, lon))
     always = [
+        edge_copy(3, 1, up, at(top_lat, top_lon + 1)),
+        edge_copy(4, 0, up + 3, at(top_lat, top_lon - 1)),
         edge_copy(1, 1, 1, at(lat, lon + 1)),
         edge_copy(2, 0, 4, at(lat, lon - 1)),
-        edge_copy(3, 1, up, at(top_lat, top_lon + 1)),
-        edge_copy(4, 0, up + 3, at(top_lat, top_lon - 1)),
     ]
     down = [
         row_copy(5, 1, 0, at(lat + 1, lon)),
         edge_copy(6, 1, 0, at(lat + 1, lon + 1)),
         edge_copy(7, 0, 3, at(lat + 1, lon - 1)),
     ]
+    for copy in always[:2]:
+        copy.start()
+
     @pl.when(is_pole)
     def _():
         turned.start()
@@ -154,7 +160,7 @@
     def _():
         above.start()
 
-    for copy in always:
+    for copy in always[2:]:
         copy.start()
 
     @pl.when(jnp.logical_not(is_last))
@@ -183,6 +189,93 @@
     def _():
         wa[1, 256:384, :] = wa[0, 0:128, :]
         wb[1, 256:384, :] = wb[0, 0:128, :]
+
+    def p1_copy(s):
+        return pltpu.make_async_remote_copy(
+            src_ref=p1s.at[s], dst_ref=p1r.at[s], send_sem=p1_send.at[s], recv_sem=p1_recv.at[s],
+            device_id=chip(q, 1 - core), device_id_type=MESH,
+        )
+
+    def p1_start(s):
+        p1s[s] = acc[s, pl.ds(pl.multiple_of((1 - core) * HALF, HALF), HALF), :].astype(BF16)
+        p1_copy(s).start()
+
+    def chunk_rows(p):
+        return pl.ds(pl.multiple_of(p * chunk, 32), chunk)
+
+    def p2_copy(s, p):
+        return pltpu.make_async_remote_copy(
+            src_ref=p2s.at[s, chunk_rows(p)], dst_ref=p2r.at[s, q], send_sem=p2_send.at[s],
+            recv_sem=p2_recv.at[s], device_id=chip(p, core), device_id_type=MESH,
+        )
+
+    def p2_start(s):
+        p1_copy(s).wait()
+        own = pl.ds(pl.multiple_of(core * HALF, HALF), HALF)
+        total = acc[s, own, :] + p1r[s].astype(F32)
+        acc[s, own, :] = total
+        p2s[s] = total.astype(BF16)
+        for k in far_first(nq):
+            p2_copy(s, lax.rem(q + k, nq)).start()
+
+    def z_copy(s, k):
+        return pltpu.make_async_remote_copy(
+            src_ref=zb.at[s, z], dst_ref=zb.at[s, z], send_sem=z_send.at[s], recv_sem=z_recv.at[s],
+            device_id=(lat, lax.rem(lon + 4 * k, nlon)), device_id_type=MESH,
+        )
+
+    def all_of(ref, sem):
+        pltpu.make_async_copy(ref, ref, sem).wait()
+
+    def z_start(s):
+        total = acc[s, pl.ds(pl.multiple_of(core * HALF + q * chunk, 32), chunk), :]
+        all_of(p2r.at[s, pl.ds(0, nq - 1)], p2_recv.at[s])
+        for k in range(1, nq):
+            total = total + p2r[s, lax.rem(q + nq - k, nq)].astype(F32)
+        zb[s, z] = total.astype(BF16)
+        for k in far_first(nz):
+            z_copy(s, k).start()
+
+    def p4_copy(s, p):
+        mine = res.at[s, core, chunk_rows(q)]
+        return pltpu.make_async_remote_copy(
+            src_ref=mine, dst_ref=mine, send_sem=p4_send.at[s], recv_sem=p4_recv.at[s],
+            device_id=chip(p, core), device_id_type=MESH,
+        )
+
+    def p4_start(s):
+        all_of(zb.at[s, pl.ds(0, nz - 1)], z_recv.at[s])
+        total = zb[s, 0].astype(F32)
+        for k in range(1, nz):
+            total = total + zb[s, k].astype(F32)
+        res[s, core, chunk_rows(q), :] = total.astype(BF16)
+        for k in far_first(nq):
+            p4_copy(s, lax.rem(q + k, nq)).start()
+
+    def p5_copy(s):
+        rows = res.at[s, core]
+        return pltpu.make_async_remote_copy(
+            src_ref=rows, dst_ref=rows, send_sem=p5_send.at[s], recv_sem=p5_recv.at[s],
+            device_id=chip(q, 1 - core), device_id_type=MESH,
+        )
+
+    def deliver(s, k):
+        rows = pl.ds(pl.multiple_of(s * 2 * HALF + k * HALF, HALF), HALF)
+        gw_o[rows, :] = res[s, k].astype(F32)
+
+    def p5_start(s):
+        all_of(res.at[s, core, pl.ds(0, HALF - chunk)], p4_recv.at[s])
+        p5_copy(s).start()
+        deliver(s, core)
+
+    def p5_finish(s):
+        p5_copy(s).wait_recv()
+        deliver(s, 1 - core)
+
+    def drain(s):
+        all_of(p2s.at[s, pl.ds(0, HALF - chunk)], p2_send.at[s])
+        all_of(zb.at[s, pl.ds(0, nz - 1)], z_send.at[s])
+        all_of(res.at[s, core, pl.ds(0, HALF - chunk)], p4_send.at[s])
 
     @pl.loop(0, ROWS)
     def _(r):
@@ -267,7 +360,10 @@
     for a in range(1, 3):
         for b in range(3):
             block = terms[128 * a : 128 * a + 128, 128 * b : 128 * b + 128]
-            acc[(3 * a + b) * 128 : (3 * a + b + 1) * 128, :] = block.T
+            acc[0, (3 * a + b - 3) * 128 : (3 * a + b - 2) * 128, :] = block.T
+
+    acc[0, 768:1024, :] = jnp.zeros((256, 128), F32)
+    p1_start(0)
 
     def grad_rows(i, taps):
         here, after = pext[i], pext[i + 1]
@@ -286,6 +382,8 @@
     def _(i):
         grad_rows(i, wa[0])
 
+    p2_start(0)
+
     edges = [jnp.concatenate([hi[side], jnp.zeros((96, 128), F32)], 0).T[0:64] for side in range(2)]
 
     def in_row(t, x, left, right):
@@ -299,8 +397,8 @@
         in_row(t, x, pltpu.roll(edges[0], 121 - t, 1), pltpu.roll(edges[1], 120 - t, 1))
 
     lhs = jnp.concatenate([in3[:, (a + 1) * 128 : (a + 16) * 128] for a in range(3)], 0)
-    acc[1152:1728, :] = dot(lhs, g_v[2:17, 0:128, :].reshape(1920, 128))
-    acc[1728:2048, :] = jnp.zeros((320, 128), F32)
+    acc[1, 384:960, :] = dot(lhs, g_v[2:17, 0:128, :].reshape(1920, 128))
+    acc[1, 960:1024, :] = jnp.zeros((64, 128), F32)
 
     @pl.when(is_pole)
     def _():
@@ -344,7 +442,7 @@
 
     first_row = both[...] + dot(gpt_top[...], act3[0:128, :])
     for b in range(3):
-        acc[b * 128 : (b + 1) * 128, :] = first_row[:, 128 * b : 128 * b + 128].T
+        acc[1, b * 128 : (b + 1) * 128, :] = first_row[:, 128 * b : 128 * b + 128].T
 
     x = row_r[0, 192:256, :].astype(F32)
     edges = [jnp.concatenate([hi[side], jnp.zeros((96, 128), F32)], 0).T[0:64] for side in range(2)]
@@ -352,49 +450,11 @@
     here = jnp.concatenate([in3[:, 0:128], in3[:, 128:256], in3[:, 256:384]], 0)
     fold = jnp.where(is_pole, in3[:, 128:256].astype(F32), 0.0).astype(BF16)
     there = jnp.concatenate([fold, jnp.zeros((384, 128), BF16)], 0)
-    acc[1152:1728, :] += dot(jnp.concatenate([here, there], 1), jnp.concatenate([g_v[1, 0:128, :], g_v[0, 0:128, :]], 0))
-
-    p1s[...] = acc[pl.ds(pl.multiple_of((1 - core) * 1024, 1024), 1024), :].astype(BF16)
-
-    def group(i):
-        return lax.rem(q // per + i, GROUPS)
-
-    def group_rows(g):
-        return pl.ds(pl.multiple_of(g * (per * chunk), 64), per * chunk)
-
-    def p1_copy(i):
-        rows = group_rows(group(i))
-        return pltpu.make_async_remote_copy(
-            src_ref=p1s.at[rows], dst_ref=p1r.at[rows], send_sem=p1_send.at[i], recv_sem=p1_recv.at[i],
-            device_id=chip(q, 1 - core), device_id_type=MESH,
-        )
-
-    order = (1, 2, 3, 0)
-    for i in order:
-        p1_copy(i).start()
-
-    def p2_copy(p):
-        rows = pl.ds(pl.multiple_of(p * chunk, 64), chunk)
-        return pltpu.make_async_remote_copy(
-            src_ref=p2s.at[rows], dst_ref=p2r.at[q], send_sem=p2_send.at[p], recv_sem=p2_recv.at[q],
-            device_id=chip(p, core), device_id_type=MESH,
-        )
-
-    for i in order:
-        p1_copy(i).wait()
-        rows = group_rows(group(i))
-        own = pl.ds(pl.multiple_of(core * 1024 + group(i) * (per * chunk), 64), per * chunk)
-        total = acc[own, :] + p1r[rows, :].astype(F32)
-        acc[own, :] = total
-        p2s[rows, :] = total.astype(BF16)
-        for j in range(per):
-            p = group(i) * per + lax.rem(q + j, per)
-            if i == 0 and j == 0:
-                continue
-            p2_copy(p).start()
-
-    @pl.loop(0, ROWS)
-    def _(r):
+    acc[1, 384:960, :] += dot(jnp.concatenate([here, there], 1), jnp.concatenate([g_v[1, 0:128, :], g_v[0, 0:128, :]], 0))
+
+    p1_start(1)
+
+    def input_row(r):
         lhs = jnp.concatenate([g_v[r + 2], g_v[r + 1], g_v[r]], 1)
         terms = dot(lhs, wb[jnp.where(r == 0, 1, 0)])
         t01, t2 = terms[:, 0:128], terms[:, 128:192]
@@ -403,64 +463,21 @@
         t2 = pltpu.roll(t2, 1, 0)[0:128].T
         gi_o[r] = (t01[0:64] + t01[64:128] + t2).astype(BF16)
 
-    total = acc[pl.ds(pl.multiple_of(core * 1024 + q * chunk, 64), chunk), :]
-    for k in range(1, nq):
-        p = lax.rem(q + nq - k, nq)
-        pltpu.make_async_copy(p2r.at[p], p2r.at[p], p2_recv.at[p]).wait()
-        total = total + p2r[p].astype(F32)
-    zb[z] = total.astype(BF16)
-
-    def z_copy(k):
-        return pltpu.make_async_remote_copy(
-            src_ref=zb.at[z], dst_ref=zb.at[z], send_sem=z_send.at[k], recv_sem=z_recv.at[z],
-            device_id=(lat, lax.rem(lon + 4 * k, nlon)), device_id_type=MESH,
-        )
-
-    for k in range(1, nz):
-        z_copy(k).start()
-    for k in range(1, nz):
-        p = lax.rem(z + nz - k, nz)
-        pltpu.make_async_copy(zb.at[p], zb.at[p], z_recv.at[p]).wait()
-    total = zb[0].astype(F32)
-    for k in range(1, nz):
-        total = total + zb[k].astype(F32)
-    mine = pl.ds(pl.multiple_of(q * chunk, 64), chunk)
-    res[core, mine, :] = total.astype(BF16)
-
-    def p4_copy(p):
-        return pltpu.make_async_remote_copy(
-            src_ref=res.at[core, mine], dst_ref=res.at[core, mine], send_sem=p4_send.at[p],
-            recv_sem=p4_recv.at[q], device_id=chip(p, core), device_id_type=MESH,
-        )
-
-    for k in range(1, nq):
-        p4_copy(lax.rem(q + k, nq)).start()
-
-    def p5_copy(p):
-        rows = pl.ds(pl.multiple_of(p * chunk, 64), chunk)
-        return pltpu.make_async_remote_copy(
-            src_ref=res.at[core, rows], dst_ref=res.at[core, rows], send_sem=p5_send.at[p],
-            recv_sem=p5_recv.at[p], device_id=chip(q, 1 - core), device_id_type=MESH,
-        )
-
-    def deliver(k, p):
-        rows = pl.ds(pl.multiple_of(p * chunk, 64), chunk)
-        gw_o[pl.ds(pl.multiple_of(k * 1024 + p * chunk, 64), chunk), :] = res[k, rows, :].astype(F32)
-
-    p5_copy(q).start()
-    deliver(core, q)
-    for k in range(1, nq):
-        p = lax.rem(q + nq - k, nq)
-        there = pl.ds(pl.multiple_of(p * chunk, 64), chunk)
-        pltpu.make_async_copy(res.at[core, there], res.at[core, there], p4_recv.at[p]).wait()
-        p5_copy(p).start()
-        deliver(core, p)
-    for k in range(nq):
-        p = lax.rem(q + nq - k, nq)
-        there = pl.ds(pl.multiple_of(p * chunk, 64), chunk)
-        other = res.at[1 - core, there]
-        pltpu.make_async_copy(other, other, p5_recv.at[p]).wait()
-        deliver(1 - core, p)
+    @pl.loop(0, ROWS // 2)
+    def _(r):
+        input_row(r)
+
+    p2_start(1)
+
+    @pl.loop(ROWS // 2, ROWS)
+    def _(r):
+        input_row(r)
+
+    z_start(0)
+    z_start(1)
+    p4_start(0)
+    p4_start(1)
+    p5_start(0)
 
     @pl.when(is_pole)
     def _():
@@ -478,20 +495,21 @@
         for copy in down:
             copy.wait_send()
 
-    for k in range(1, nq):
-        p2_copy(lax.rem(q + k, nq)).wait_send()
-        p4_copy(lax.rem(q + k, nq)).wait_send()
-    for k in range(1, nz):
-        z_copy(k).wait_send()
-    for p in range(nq):
-        p5_copy(p).wait_send()
+    drain(0)
+    p5_finish(0)
+    p5_start(1)
+    drain(1)
+    p5_finish(1)
+    p5_copy(0).wait_send()
+    p5_copy(1).wait_send()
 
 
 def write_out(gi_v, gw_v, gi_o, gw1_o, gw2_o, sem):
     copies = [
-        pltpu.make_async_copy(gw_v.at[pl.ds(0, 1152)], gw2_o, sem.at[0]),
-        pltpu.make_async_copy(gw_v.at[pl.ds(1152, 576)], gw1_o, sem.at[1]),
-        pltpu.make_async_copy(gi_v, gi_o, sem.at[2]),
+        pltpu.make_async_copy(gw_v.at[pl.ds(0, 768)], gw2_o.at[pl.ds(384, 768)], sem.at[0]),
+        pltpu.make_async_copy(gw_v.at[pl.ds(1024, 384)], gw2_o.at[pl.ds(0, 384)], sem.at[1]),
+        pltpu.make_async_copy(gw_v.at[pl.ds(1408, 576)], gw1_o, sem.at[2]),
+        pltpu.make_async_copy(gi_v, gi_o, sem.at[3]),
     ]
     for copy in copies:
         copy.start()
@@ -501,7 +519,7 @@
 
 def section(nlat, nlon, inputs, pre_first, grad_out, w_first, w_second):
     nq, nz = nlat * 2, nlon // 4
-    chunk = 1024 // nq
+    chunk = HALF // nq
     hbm = pl.BlockSpec(memory_space=pltpu.HBM)
     vmem = pltpu.VMEM
     dma = pltpu.SemaphoreType.DMA
@@ -536,20 +554,20 @@
             vmem((18, WIDE, 128), BF16),
             vmem((2, WIDE, 128), F32),
             vmem((128, 384), F32),
-            vmem((2048, 128), F32),
-            vmem((1024, 128), BF16),
-            vmem((1024, 128), BF16),
-            vmem((1024, 128), BF16),
-            vmem((nq, chunk, 128), BF16),
-            vmem((nz, chunk, 128), BF16),
-            vmem((2, 1024, 128), BF16),
+            vmem((2, 2 * HALF, 128), F32),
+            vmem((2, HALF, 128), BF16),
+            vmem((2, HALF, 128), BF16),
+            vmem((2, HALF, 128), BF16),
+            vmem((2, nq, chunk, 128), BF16),
+            vmem((2, nz, chunk, 128), BF16),
+            vmem((2, 2, HALF, 128), BF16),
             dma((5,)),
             dma((8,)), dma((8,)),
-            dma((GROUPS,)), dma((GROUPS,)),
-            dma((nq,)), dma((nq,)),
-            dma((nz,)), dma((nz,)),
-            dma((nq,)), dma((nq,)),
-            dma((nq,)), dma((nq,)),
+            dma((2,)), dma((2,)),
+            dma((2,)), dma((2,)),
+            dma((2,)), dma((2,)),
+            dma((2,)), dma((2,)),
+            dma((2,)), dma((2,)),
         ],
         compiler_params=pltpu.CompilerParams(
             collective_id=0, has_side_effects=True, vmem_limit_bytes=40 * 1024 * 1024
@@ -576,7 +594,7 @@
         ),
         in_specs=[pl.BlockSpec(memory_space=vmem)] * 2,
         out_specs=(pl.BlockSpec(memory_space=pl.ANY),) * 3,
-        scratch_shapes=[dma((3,))],
+        scratch_shapes=[dma((4,))],
         compiler_params=pltpu.CompilerParams(vmem_limit_bytes=16 * 1024 * 1024),
     )(gi, gw)
     return (

time: 44.5 us -> 41.7 us (0.937)
  Pallas kernels: 43.8 us -> 40.9 us
    pallas_call x1, Pallas kernels: 42.7 us -> 39.9 us  [section(): pl.pallas_call(functools.partial(kernel, nlat, nlon), out_shape=(vmem((RO...]
where the time goes in v3:
time: 41.7 us; the launch traced here: 41.6 us
  Pallas kernels  40.9 us (98%)
  between operations  0.64 us (2%)
    pallas_call x1, Pallas kernels, section(): pl.pallas_call(functools.partial(kernel, nlat, nlon), out_shape=(vmem((RO...  39.9 us
    pallas_call x1, Pallas kernels, section(): pl.pallas_call(write_out, out_shape=(jax.ShapeDtypeStruct((ROWS, C0, COLS...  1.03 us

profile of v3, /device:TPU:1, one launch (start us, length us, event | category | flops | bytes accessed | tf_op | source)
XLA Modules:
  0.0 41.6 jit_solution(9405226374578068490)
XLA Ops:
  0.6 39.9 %shard_map.76 = (bf16[16,64,128]{2,1,0:T(8,128)(2,1)S(1)}, f32[2048,128]{1,0:T(8,128)S(1)}) custom-call(bf16[16,128,128]{2,1,0:T(8,128)(2,1)} %pre_h.1, bf16[16,64,128]{2,1,0:T(8,128)(2,1)} %bitcast.9, bf16[8,64,128]{2,1,0:T(8,128)(2,1)} %go_h.1, bf16[9,64,128]{2,1,0:T(8,128)(2,1)} %bitcast.11, bf16[9,128,128]{2,1,0:T(8,128)(2,1)} %bitcast.7), custom_call_target="tpu_custom_call" | custom-call | flops 1800000000 | bytes 3000000 | tf_op jit(solution)/shard_map/pallas_call | solution.py:526
  40.6 1.0 %shard_map.77 = (bf16[16,64,128]{2,1,0:T(8,128)(2,1)}, f32[576,128]{1,0:T(8,128)}, f32[1152,128]{1,0:T(8,128)}) custom-call(bf16[16,64,128]{2,1,0:T(8,128)(2,1)S(1)} %get-tuple-element.8.gi_v, f32[2048,128]{1,0:T(8,128)S(1)} %get-tuple-element.9.gw_v), custom_call_target="tpu_custom_call" | custom-call | tf_op jit(solution)/shard_map/pallas_call | solution.py:588

commit v4 on v3

--- a/solution.py
+++ b/solution.py
@@ -40,7 +40,7 @@
     gi_o, gw_o,
     pre_v, in_v, go_v, w1_v, w2_v, wa, wb,
     e_s, row_s, e_r, row_r, hc, hs, hg, hi,
-    act_f, slope_f, act3, pext, gpt, gpt_top, in3, g_v, ga_f, both,
+    slope_f, act3, pext, gpt, gpt_top, gpt_side, in3, g_v, ga_f, both,
     acc, p1s, p1r, p2s, p2r, zb, res,
     load_sem, halo_send, halo_recv, p1_send, p1_recv, p2_send, p2_recv,
     z_send, z_recv, p4_send, p4_recv, p5_send, p5_recv,
@@ -277,10 +277,18 @@
         all_of(zb.at[s, pl.ds(0, nz - 1)], z_send.at[s])
         all_of(res.at[s, core, pl.ds(0, HALF - chunk)], p4_send.at[s])
 
-    @pl.loop(0, ROWS)
+    column = lax.broadcasted_iota(jnp.int32, (128, 128), 0)
+
+    def act_row(t, x, left, right):
+        rows = pl.ds(pl.multiple_of(t * 128, 128), 128)
+        act3[rows, 0:128] = jnp.where(column == 0, left, pltpu.roll(x, 1, 0)).astype(BF16)
+        act3[rows, 128:256] = x.astype(BF16)
+        act3[rows, 256:384] = jnp.where(column == 127, right, pltpu.roll(x, 127, 0)).astype(BF16)
+
+    @pl.loop(0, ROWS, unroll=2)
     def _(r):
         act, slope = gelu_parts(pre_v[r].astype(F32))
-        act_f[r + 1, 0:128, :] = act
+        act_row(r + 1, act, 0.0, 0.0)
         slope_f[r + 1, 0:128, :] = slope
 
     copies = lax.broadcasted_iota(jnp.int32, (64, 128), 1) // 2
@@ -293,6 +301,43 @@
         ).astype(BF16)
         gpt[:, (2 * i + 2) * 128 : (2 * i + 3) * 128] = t
         gpt[:, (2 * i + 3) * 128 : (2 * i + 4) * 128] = t
+
+    corner = jnp.concatenate([e_s[0, 16:32, :], e_s[1, 16:32, :]], 0)
+    place = lax.broadcasted_iota(jnp.int32, (32, 128), 1)
+    source = lax.broadcasted_iota(jnp.int32, (32, 128), 0)
+    for a in range(3):
+        row = place % 32 - 7 - a
+        chosen = jnp.logical_and(
+            jnp.logical_and(row >= 0, row < ROWS), place // 32 * 16 + (row + 16) // 2 - 8 == source
+        )
+        chosen = jnp.where(chosen, 0.25, 0.0).astype(BF16)
+        gpt_side[128 * a : 128 * a + 128, :] = lax.dot_general(
+            corner, chosen, (((0,), (0,)), ((), ())), preferred_element_type=F32
+        ).astype(BF16)
+
+    lhs = jnp.concatenate([gpt[:, (3 - a) * 128 : (3 - a) * 128 + 2048] for a in range(3)], 0)
+    both[...] = dot(lhs, act3[128 : 17 * 128, :])
+
+    def grad_rows(i, taps):
+        here, after = pext[i], pext[i + 1]
+        lhs = jnp.concatenate(
+            [jnp.concatenate([after, here, here], 1), jnp.concatenate([after, after, here], 1)], 0
+        )
+        terms = dot(lhs, taps)
+        for s in range(2):
+            part = terms[PWIDE * s : PWIDE * (s + 1)]
+            t0, t1, t2 = part[:, 0:128], part[:, 128:256], part[:, 256:384]
+            ga_f[2 * i + s, pl.ds(0, PWIDE, stride=2), :] = t0 + t1 + pltpu.roll(t2, 1, 0)
+            ga_f[2 * i + s, pl.ds(1, PWIDE, stride=2), :] = pltpu.roll(t0, PWIDE - 1, 0) + t1 + t2
+            g_v[2 * i + s] = (ga_f[2 * i + s] * slope_f[2 * i + s]).astype(BF16)
+
+    for i in range(1, 9):
+        pext[i, 0:64, :] = (0.25 * go_v[i - 1].astype(F32)).astype(BF16)
+        pext[i, 64:80, :] = jnp.zeros((16, 128), BF16)
+
+    @pl.loop(1, 8, unroll=7)
+    def _(i):
+        grad_rows(i, wa[0])
 
     def arrived(slot):
         dst = e_r.at[slot] if slot < 6 else row_r.at[slot - 6]
@@ -322,65 +367,60 @@
         hi[side, 8:24, :] = mid[32:48]
         hi[side, 24:32, :] = jnp.broadcast_to(low[32:33], (8, 128))
     act, slope = gelu_parts(row_r[1, 0:128, :].astype(F32))
-    act_f[17, 0:128, :] = act
+    act_row(17, act, 0.0, 0.0)
     slope_f[17, 0:128, :] = slope * keep
 
     def sides(t):
         scale = keep if t == 17 else 1.0
         for side, place in enumerate((152, 128)):
-            act_f[t, place : place + 8, :] = jnp.broadcast_to(hc[side, t + 7 : t + 8, :], (8, 128))
             slope_f[t, place : place + 8, :] = scale * jnp.broadcast_to(hs[side, t + 7 : t + 8, :], (8, 128))
 
-    def pooled(i, part):
-        pext[i, 0:64, :] = (0.25 * part.astype(F32)).astype(BF16)
+    def pooled(i):
         left = jnp.broadcast_to(hg[0, i + 7 : i + 8, :], (16, 128))
         right = jnp.broadcast_to(hg[1, i + 7 : i + 8, :], (16, 128))
         tile = jnp.where(sub == 0, right, jnp.where(sub == 15, left, 0.0))
         pext[i, 64:80, :] = tile.astype(BF16)
 
-    def act_row(t):
-        x = act_f[t]
-        rows = pl.ds(pl.multiple_of(t * 128, 128), 128)
-        act3[rows, 0:128] = pltpu.roll(x, 1, 0)[0:128].astype(BF16)
-        act3[rows, 128:256] = x[0:128].astype(BF16)
-        act3[rows, 256:384] = pltpu.roll(x, WIDE - 1, 0)[0:128].astype(BF16)
-
-    for t in range(1, 18):
-        sides(t)
-    for i in range(1, 10):
-        pooled(i, go_v[i - 1] if i < 9 else row_r[1, 128:192, :])
-
-    @pl.loop(1, 18)
-    def _(t):
-        act_row(t)
-
-    lhs = jnp.concatenate([gpt[:, (3 - a) * 128 : (3 - a) * 128 + 17 * 128] for a in range(3)], 0)
-    terms = dot(lhs, act3[128:2304, :])
-    both[...] = terms[0:128]
+    below = jnp.logical_and(
+        lax.broadcasted_iota(jnp.int32, (32, 128), 0) >= 8, lax.broadcasted_iota(jnp.int32, (32, 128), 0) < 25
+    )
+    act3[2304:2432, :] = jnp.zeros((128, 384), BF16)
+    act3[2304:2336, 0:128] = jnp.where(below, hc[0], 0.0).astype(BF16)
+    act3[2336:2368, 256:384] = jnp.where(below, hc[1], 0.0).astype(BF16)
+    lhs = jnp.concatenate(
+        [jnp.concatenate([gpt[:, (19 - a) * 128 : (20 - a) * 128] for a in range(3)], 0), gpt_side[...]], 1
+    )
+    terms = both[...] + dot(lhs, act3[2176:2432, :])
     for a in range(1, 3):
         for b in range(3):
             block = terms[128 * a : 128 * a + 128, 128 * b : 128 * b + 128]
             acc[0, (3 * a + b - 3) * 128 : (3 * a + b - 2) * 128, :] = block.T
-
+    both[0:128, :] = terms[0:128]
     acc[0, 768:1024, :] = jnp.zeros((256, 128), F32)
     p1_start(0)
 
-    def grad_rows(i, taps):
-        here, after = pext[i], pext[i + 1]
-        lhs = jnp.concatenate(
-            [jnp.concatenate([after, here, here], 1), jnp.concatenate([after, after, here], 1)], 0
-        )
-        terms = dot(lhs, taps)
-        for s in range(2):
-            part = terms[PWIDE * s : PWIDE * (s + 1)]
-            t0, t1, t2 = part[:, 0:128], part[:, 128:256], part[:, 256:384]
-            ga_f[s, pl.ds(0, PWIDE, stride=2), :] = t0 + t1 + pltpu.roll(t2, 1, 0)
-            ga_f[s, pl.ds(1, PWIDE, stride=2), :] = pltpu.roll(t0, PWIDE - 1, 0) + t1 + t2
-            g_v[2 * i + s] = (ga_f[s] * slope_f[2 * i + s]).astype(BF16)
-
-    @pl.loop(1, 9)
-    def _(i):
-        grad_rows(i, wa[0])
+    for t in range(1, 18):
+        sides(t)
+    pext[9, 0:64, :] = (0.25 * row_r[1, 128:192, :].astype(F32)).astype(BF16)
+    for i in range(1, 10):
+        pooled(i)
+    tiles = [pext[i, 64:80, :] for i in range(1, 9)]
+    lhs = jnp.concatenate(
+        [
+            jnp.concatenate([tiles[(t + 2) // 2 - 1], tiles[(t + 1) // 2 - 1], tiles[t // 2 - 1]], 1)
+            for t in range(2, 16)
+        ],
+        0,
+    )
+    terms = dot(lhs, wa[0])
+    for t in range(2, 16):
+        part = terms[16 * (t - 2) : 16 * (t - 1)]
+        t0, t1, t2 = part[:, 0:128], part[:, 128:256], part[:, 256:384]
+        for first, at_row, more in ((0, 0, t2[15:16]), (112, 15, t0[0:1]), (128, 0, (t0 + t1)[0:1]), (144, 15, (t1 + t2)[15:16])):
+            more = jnp.where(sub == at_row, jnp.broadcast_to(more, (16, 128)), 0.0)
+            cells = slice(first, first + 16)
+            g_v[t, cells, :] = ((ga_f[t, cells, :] + more) * slope_f[t, cells, :]).astype(BF16)
+    grad_rows(8, wa[0])
 
     p2_start(0)
 
@@ -424,13 +464,13 @@
         hg[side, 0:8, :] = 0.25 * pick(16, 23)
         hi[side, 0:8, :] = jnp.where(is_pole, 0.0, pick(32, 47))
     act, slope = gelu_parts(row_r[0, 0:128, :].astype(F32))
-    act_f[0, 0:128, :] = act
     slope_f[0, 0:128, :] = slope
     sides(0)
-    pooled(0, row_r[0, 128:192, :])
+    pext[0, 0:64, :] = (0.25 * row_r[0, 128:192, :].astype(F32)).astype(BF16)
+    pooled(0)
     grad_rows(0, wa[1])
 
-    act_row(0)
+    act_row(0, act, jnp.broadcast_to(hc[0, 7:8, :], (128, 128)), jnp.broadcast_to(hc[1, 7:8, :], (128, 128)))
     top_go = lax.dot_general(
         row_r[0, 128:192, :], copies, (((0,), (0,)), ((), ())), preferred_element_type=F32
     ).astype(BF16)
@@ -438,9 +478,14 @@
 
     @pl.when(is_pole)
     def _():
-        act3[0:128, :] = act3[128:256, :]
-
-    first_row = both[...] + dot(gpt_top[...], act3[0:128, :])
+        act_row(
+            0,
+            act3[128:256, 128:256].astype(F32),
+            jnp.broadcast_to(hc[0, 8:9, :], (128, 128)),
+            jnp.broadcast_to(hc[1, 8:9, :], (128, 128)),
+        )
+
+    first_row = both[0:128, :] + dot(gpt_top[...], act3[0:128, :])
     for b in range(3):
         acc[1, b * 128 : (b + 1) * 128, :] = first_row[:, 128 * b : 128 * b + 128].T
 
@@ -463,13 +508,13 @@
         t2 = pltpu.roll(t2, 1, 0)[0:128].T
         gi_o[r] = (t01[0:64] + t01[64:128] + t2).astype(BF16)
 
-    @pl.loop(0, ROWS // 2)
+    @pl.loop(0, ROWS // 2, unroll=2)
     def _(r):
         input_row(r)
 
     p2_start(1)
 
-    @pl.loop(ROWS // 2, ROWS)
+    @pl.loop(ROWS // 2, ROWS, unroll=2)
     def _(r):
         input_row(r)
 
@@ -545,15 +590,15 @@
             vmem((2, 24, 128), F32),
             vmem((2, 32, 128), F32),
             vmem((18, WIDE, 128), F32),
-            vmem((18, WIDE, 128), F32),
-            vmem((18 * 128, 384), BF16),
+            vmem((19 * 128, 384), BF16),
             vmem((10, PWIDE, 128), BF16),
             vmem((128, 20 * 128), BF16),
             vmem((128, 128), BF16),
+            vmem((384, 128), BF16),
             vmem((192, 18 * 128), BF16),
             vmem((18, WIDE, 128), BF16),
-            vmem((2, WIDE, 128), F32),
-            vmem((128, 384), F32),
+            vmem((18, WIDE, 128), F32),
+            vmem((384, 384), F32),
             vmem((2, 2 * HALF, 128), F32),
             vmem((2, HALF, 128), BF16),
             vmem((2, HALF, 128), BF16),

time: 41.7 us -> 39.2 us (0.940)
  Pallas kernels: 40.9 us -> 38.4 us
    pallas_call x1, Pallas kernels: 39.9 us -> 37.4 us  [section(): pl.pallas_call(functools.partial(kernel, nlat, nlon), out_shape=(vmem((RO...]
where the time goes in v4:
time: 39.2 us; the launch traced here: 39.1 us
  Pallas kernels  38.4 us (98%)
  between operations  0.64 us (2%)
    pallas_call x1, Pallas kernels, section(): pl.pallas_call(functools.partial(kernel, nlat, nlon), out_shape=(vmem((RO...  37.4 us
    pallas_call x1, Pallas kernels, section(): pl.pallas_call(write_out, out_shape=(jax.ShapeDtypeStruct((ROWS, C0, COLS...  1.03 us

profile of v4, /device:TPU:1, one launch (start us, length us, event | category | flops | bytes accessed | tf_op | source)
XLA Modules:
  0.0 39.1 jit_solution(16690581398838999364)
XLA Ops:
  0.6 37.4 %shard_map.76 = (bf16[16,64,128]{2,1,0:T(8,128)(2,1)S(1)}, f32[2048,128]{1,0:T(8,128)S(1)}) custom-call(bf16[16,128,128]{2,1,0:T(8,128)(2,1)} %pre_h.1, bf16[16,64,128]{2,1,0:T(8,128)(2,1)} %bitcast.9, bf16[8,64,128]{2,1,0:T(8,128)(2,1)} %go_h.1, bf16[9,64,128]{2,1,0:T(8,128)(2,1)} %bitcast.11, bf16[9,128,128]{2,1,0:T(8,128)(2,1)} %bitcast.7), custom_call_target="tpu_custom_call" | custom-call | flops 1800000000 | bytes 3000000 | tf_op jit(solution)/shard_map/pallas_call | solution.py:571
  38.0 1.0 %shard_map.77 = (bf16[16,64,128]{2,1,0:T(8,128)(2,1)}, f32[576,128]{1,0:T(8,128)}, f32[1152,128]{1,0:T(8,128)}) custom-call(bf16[16,64,128]{2,1,0:T(8,128)(2,1)S(1)} %get-tuple-element.8.gi_v, f32[2048,128]{1,0:T(8,128)S(1)} %get-tuple-element.9.gw_v), custom_call_target="tpu_custom_call" | custom-call | tf_op jit(solution)/shard_map/pallas_call | solution.py:633

commit v5 on v4

--- a/solution.py
+++ b/solution.py
@@ -40,7 +40,7 @@
     gi_o, gw_o,
     pre_v, in_v, go_v, w1_v, w2_v, wa, wb,
     e_s, row_s, e_r, row_r, hc, hs, hg, hi,
-    slope_f, act3, pext, gpt, gpt_top, gpt_side, in3, g_v, ga_f, both,
+    slope_f, act3, pext, gpt, gpt_top, gpt_side, in3, in_edge, g_edge, g_v, ga_f, both,
     acc, p1s, p1r, p2s, p2r, zb, res,
     load_sem, halo_send, halo_recv, p1_send, p1_recv, p2_send, p2_recv,
     z_send, z_recv, p4_send, p4_recv, p5_send, p5_recv,
@@ -285,7 +285,7 @@
         act3[rows, 128:256] = x.astype(BF16)
         act3[rows, 256:384] = jnp.where(column == 127, right, pltpu.roll(x, 127, 0)).astype(BF16)
 
-    @pl.loop(0, ROWS, unroll=2)
+    @pl.loop(0, ROWS, unroll=4)
     def _(r):
         act, slope = gelu_parts(pre_v[r].astype(F32))
         act_row(r + 1, act, 0.0, 0.0)
@@ -338,6 +338,32 @@
     @pl.loop(1, 8, unroll=7)
     def _(i):
         grad_rows(i, wa[0])
+
+    def in_row(t, x, left, right):
+        cells = slice(128 * t, 128 * t + 128)
+        in3[0:64, cells] = jnp.where(lane == 0, left, pltpu.roll(x, 1, 1)).astype(BF16)
+        in3[64:128, cells] = x.astype(BF16)
+        in3[128:192, cells] = jnp.where(lane == 127, right, pltpu.roll(x, 127, 1)).astype(BF16)
+
+    for t in range(1, 17):
+        in_row(t, in_v[t - 1].astype(F32), 0.0, 0.0)
+
+    inner = jnp.where(jnp.logical_and(column > 0, column < 127), 1.0, 0.0)
+    lhs = jnp.concatenate([in3[:, (a + 1) * 128 : (a + 15) * 128] for a in range(3)], 0)
+    rhs = [(g_v[t, 0:128, :].astype(F32) * inner).astype(BF16) for t in range(2, 16)]
+    acc[1, 384:960, :] = dot(lhs, jnp.concatenate(rhs, 0))
+    acc[1, 960:1024, :] = jnp.zeros((64, 128), F32)
+
+    g_edge[...] = jnp.zeros((128, 128), F32)
+    for b, (low, high) in enumerate(((None, 126), (0, 127), (1, None))):
+        edge = jnp.zeros((C0, 128), F32)
+        for r in range(ROWS):
+            x = in_v[r].astype(F32)
+            if low is not None:
+                edge = jnp.where(lane == 8 + r, pltpu.roll(x, 8 + r - low, 1), edge)
+            if high is not None:
+                edge = jnp.where(lane == 40 + r, pltpu.roll(x, (40 + r - high) % 128, 1), edge)
+        in_edge[b] = edge
 
     def arrived(slot):
         dst = e_r.at[slot] if slot < 6 else row_r.at[slot - 6]
@@ -419,26 +445,26 @@
         for first, at_row, more in ((0, 0, t2[15:16]), (112, 15, t0[0:1]), (128, 0, (t0 + t1)[0:1]), (144, 15, (t1 + t2)[15:16])):
             more = jnp.where(sub == at_row, jnp.broadcast_to(more, (16, 128)), 0.0)
             cells = slice(first, first + 16)
-            g_v[t, cells, :] = ((ga_f[t, cells, :] + more) * slope_f[t, cells, :]).astype(BF16)
+            grad = (ga_f[t, cells, :] + more) * slope_f[t, cells, :]
+            g_v[t, cells, :] = grad.astype(BF16)
+            if first == 0:
+                g_edge[t + 7 : t + 8, :] = grad[0:1]
+            if first == 112:
+                g_edge[t + 39 : t + 40, :] = grad[15:16]
     grad_rows(8, wa[0])
 
-    p2_start(0)
-
     edges = [jnp.concatenate([hi[side], jnp.zeros((96, 128), F32)], 0).T[0:64] for side in range(2)]
-
-    def in_row(t, x, left, right):
-        cells = slice(128 * t, 128 * t + 128)
-        in3[0:64, cells] = jnp.where(lane == 0, left, pltpu.roll(x, 1, 1)).astype(BF16)
-        in3[64:128, cells] = x.astype(BF16)
-        in3[128:192, cells] = jnp.where(lane == 127, right, pltpu.roll(x, 127, 1)).astype(BF16)
-
-    for t in range(1, 18):
+    for t in (1, 2, 15, 16, 17):
         x = (in_v[t - 1] if t < 17 else row_r[1, 192:256, :]).astype(F32)
         in_row(t, x, pltpu.roll(edges[0], 121 - t, 1), pltpu.roll(edges[1], 120 - t, 1))
-
-    lhs = jnp.concatenate([in3[:, (a + 1) * 128 : (a + 16) * 128] for a in range(3)], 0)
-    acc[1, 384:960, :] = dot(lhs, g_v[2:17, 0:128, :].reshape(1920, 128))
-    acc[1, 960:1024, :] = jnp.zeros((64, 128), F32)
+    beside = [
+        jnp.where(lane < 32, edges[0], in_edge[0]),
+        in_edge[1],
+        jnp.where(lane < 32, in_edge[2], pltpu.roll(edges[1], 32, 1)),
+    ]
+    beside = jnp.concatenate(
+        [(pltpu.roll(x, (1 - a) % 128, 1) if a != 1 else x).astype(BF16) for a in range(3) for x in beside], 0
+    )
 
     @pl.when(is_pole)
     def _():
@@ -495,9 +521,12 @@
     here = jnp.concatenate([in3[:, 0:128], in3[:, 128:256], in3[:, 256:384]], 0)
     fold = jnp.where(is_pole, in3[:, 128:256].astype(F32), 0.0).astype(BF16)
     there = jnp.concatenate([fold, jnp.zeros((384, 128), BF16)], 0)
-    acc[1, 384:960, :] += dot(jnp.concatenate([here, there], 1), jnp.concatenate([g_v[1, 0:128, :], g_v[0, 0:128, :]], 0))
+    last = jnp.concatenate([in3[:, 15 * 128 : 16 * 128], in3[:, 16 * 128 : 17 * 128], in3[:, 17 * 128 : 18 * 128]], 0)
+    rhs = [g_v[1, 0:128, :], g_v[0, 0:128, :], g_v[16, 0:128, :], g_edge[...].astype(BF16)]
+    acc[1, 384:960, :] += dot(jnp.concatenate([here, there, last, beside], 1), jnp.concatenate(rhs, 0))
 
     p1_start(1)
+    p2_start(0)
 
     def input_row(r):
         lhs = jnp.concatenate([g_v[r + 2], g_v[r + 1], g_v[r]], 1)
@@ -508,13 +537,13 @@
         t2 = pltpu.roll(t2, 1, 0)[0:128].T
         gi_o[r] = (t01[0:64] + t01[64:128] + t2).astype(BF16)
 
-    @pl.loop(0, ROWS // 2, unroll=2)
+    @pl.loop(0, ROWS // 2, unroll=4)
     def _(r):
         input_row(r)
 
     p2_start(1)
 
-    @pl.loop(ROWS // 2, ROWS, unroll=2)
+    @pl.loop(ROWS // 2, ROWS, unroll=4)
     def _(r):
         input_row(r)
 
@@ -596,6 +625,8 @@
             vmem((128, 128), BF16),
             vmem((384, 128), BF16),
             vmem((192, 18 * 128), BF16),
+            vmem((3, C0, 128), F32),
+            vmem((128, 128), F32),
             vmem((18, WIDE, 128), BF16),
             vmem((18, WIDE, 128), F32),
             vmem((384, 384), F32),

time: 39.2 us -> 38.1 us (0.972)
  Pallas kernels: 38.4 us -> 37.3 us
    pallas_call x1, Pallas kernels: 37.4 us -> 36.3 us  [section(): pl.pallas_call(functools.partial(kernel, nlat, nlon), out_shape=(vmem((RO...]
where the time goes in v5:
time: 38.1 us; the launch traced here: 38 us
  Pallas kernels  37.3 us (98%)
  between operations  0.64 us (2%)
    pallas_call x1, Pallas kernels, section(): pl.pallas_call(functools.partial(kernel, nlat, nlon), out_shape=(vmem((RO...  36.3 us
    pallas_call x1, Pallas kernels, section(): pl.pallas_call(write_out, out_shape=(jax.ShapeDtypeStruct((ROWS, C0, COLS...  1.03 us

profile of v5, /device:TPU:1, one launch (start us, length us, event | category | flops | bytes accessed | tf_op | source)
XLA Modules:
  0.0 38.0 jit_solution(13051113908826686450)
XLA Ops:
  0.6 36.3 %shard_map.76 = (bf16[16,64,128]{2,1,0:T(8,128)(2,1)S(1)}, f32[2048,128]{1,0:T(8,128)S(1)}) custom-call(bf16[16,128,128]{2,1,0:T(8,128)(2,1)} %pre_h.1, bf16[16,64,128]{2,1,0:T(8,128)(2,1)} %bitcast.9, bf16[8,64,128]{2,1,0:T(8,128)(2,1)} %go_h.1, bf16[9,64,128]{2,1,0:T(8,128)(2,1)} %bitcast.11, bf16[9,128,128]{2,1,0:T(8,128)(2,1)} %bitcast.7), custom_call_target="tpu_custom_call" | custom-call | flops 1800000000 | bytes 3000000 | tf_op jit(solution)/shard_map/pallas_call | solution.py:600
  36.9 1.0 %shard_map.77 = (bf16[16,64,128]{2,1,0:T(8,128)(2,1)}, f32[576,128]{1,0:T(8,128)}, f32[1152,128]{1,0:T(8,128)}) custom-call(bf16[16,64,128]{2,1,0:T(8,128)(2,1)S(1)} %get-tuple-element.8.gi_v, f32[2048,128]{1,0:T(8,128)S(1)} %get-tuple-element.9.gw_v), custom_call_target="tpu_custom_call" | custom-call | tf_op jit(solution)/shard_map/pallas_call | solution.py:664

commit v6 on v5

--- a/solution.py
+++ b/solution.py
@@ -40,7 +40,7 @@
     gi_o, gw_o,
     pre_v, in_v, go_v, w1_v, w2_v, wa, wb,
     e_s, row_s, e_r, row_r, hc, hs, hg, hi,
-    slope_f, act3, pext, gpt, gpt_top, gpt_side, in3, in_edge, g_edge, g_v, ga_f, both,
+    slope_f, act3, pext, gpt, gpt_top, gpt_side, in3, in_edge, g_edge, wide, g_v, ga_f, both,
     acc, p1s, p1r, p2s, p2r, zb, res,
     load_sem, halo_send, halo_recv, p1_send, p1_recv, p2_send, p2_recv,
     z_send, z_recv, p4_send, p4_recv, p5_send, p5_recv,
@@ -78,18 +78,22 @@
     top_lon = jnp.where(is_pole, lon + half, lon)
     for d in (-1, 0, 1):
         greet(at(top_lat, top_lon + d))
-    for k in far_first(nz):
+    for k in far_first(nz)[:1]:
         greet((lat, lax.rem(lon + 4 * k, nlon)))
-    for k in far_first(nq):
+    for k in far_first(nq)[:3]:
         greet(chip(lax.rem(q + k, nq), core))
     for d in (-1, 1):
         greet(at(lat, lon + d))
 
     @pl.when(jnp.logical_not(is_last))
     def _():
-        for d in (-1, 0, 1):
+        for d in (-1, 1, 0):
             greet(at(lat + 1, lon + d))
 
+    for k in far_first(nz)[1:]:
+        greet((lat, lax.rem(lon + 4 * k, nlon)))
+    for k in far_first(nq)[3:]:
+        greet(chip(lax.rem(q + k, nq), core))
     greet(chip(q, 1 - core))
 
     loads[0].wait()
@@ -442,29 +446,15 @@
     for t in range(2, 16):
         part = terms[16 * (t - 2) : 16 * (t - 1)]
         t0, t1, t2 = part[:, 0:128], part[:, 128:256], part[:, 256:384]
-        for first, at_row, more in ((0, 0, t2[15:16]), (112, 15, t0[0:1]), (128, 0, (t0 + t1)[0:1]), (144, 15, (t1 + t2)[15:16])):
-            more = jnp.where(sub == at_row, jnp.broadcast_to(more, (16, 128)), 0.0)
-            cells = slice(first, first + 16)
-            grad = (ga_f[t, cells, :] + more) * slope_f[t, cells, :]
-            g_v[t, cells, :] = grad.astype(BF16)
-            if first == 0:
-                g_edge[t + 7 : t + 8, :] = grad[0:1]
-            if first == 112:
-                g_edge[t + 39 : t + 40, :] = grad[15:16]
+        low = (ga_f[t, 0:1, :] + t2[15:16]) * slope_f[t, 0:1, :]
+        high = (ga_f[t, 127:128, :] + t0[0:1]) * slope_f[t, 127:128, :]
+        g_edge[t + 7 : t + 8, :] = low
+        g_edge[t + 39 : t + 40, :] = high
+        wide[t, 0:1, :] = t2[15:16]
+        wide[t, 1:2, :] = t0[0:1]
+        wide[t, 2:3, :] = (t0 + t1)[0:1]
+        wide[t, 3:4, :] = (t1 + t2)[15:16]
     grad_rows(8, wa[0])
-
-    edges = [jnp.concatenate([hi[side], jnp.zeros((96, 128), F32)], 0).T[0:64] for side in range(2)]
-    for t in (1, 2, 15, 16, 17):
-        x = (in_v[t - 1] if t < 17 else row_r[1, 192:256, :]).astype(F32)
-        in_row(t, x, pltpu.roll(edges[0], 121 - t, 1), pltpu.roll(edges[1], 120 - t, 1))
-    beside = [
-        jnp.where(lane < 32, edges[0], in_edge[0]),
-        in_edge[1],
-        jnp.where(lane < 32, in_edge[2], pltpu.roll(edges[1], 32, 1)),
-    ]
-    beside = jnp.concatenate(
-        [(pltpu.roll(x, (1 - a) % 128, 1) if a != 1 else x).astype(BF16) for a in range(3) for x in beside], 0
-    )
 
     @pl.when(is_pole)
     def _():
@@ -496,28 +486,36 @@
     pooled(0)
     grad_rows(0, wa[1])
 
-    act_row(0, act, jnp.broadcast_to(hc[0, 7:8, :], (128, 128)), jnp.broadcast_to(hc[1, 7:8, :], (128, 128)))
+    cells, left, right = (
+        jnp.where(is_pole, own, above)
+        for own, above in (
+            (act3[128:256, 128:256].astype(F32), act),
+            (hc[0, 8:9, :], hc[0, 7:8, :]),
+            (hc[1, 8:9, :], hc[1, 7:8, :]),
+        )
+    )
+    act_row(0, cells, jnp.broadcast_to(left, (128, 128)), jnp.broadcast_to(right, (128, 128)))
     top_go = lax.dot_general(
         row_r[0, 128:192, :], copies, (((0,), (0,)), ((), ())), preferred_element_type=F32
     ).astype(BF16)
     gpt_top[...] = jnp.where(is_pole, top_go.astype(F32), gpt[:, 256:384].astype(F32)).astype(BF16)
 
-    @pl.when(is_pole)
-    def _():
-        act_row(
-            0,
-            act3[128:256, 128:256].astype(F32),
-            jnp.broadcast_to(hc[0, 8:9, :], (128, 128)),
-            jnp.broadcast_to(hc[1, 8:9, :], (128, 128)),
-        )
-
     first_row = both[0:128, :] + dot(gpt_top[...], act3[0:128, :])
     for b in range(3):
         acc[1, b * 128 : (b + 1) * 128, :] = first_row[:, 128 * b : 128 * b + 128].T
 
-    x = row_r[0, 192:256, :].astype(F32)
     edges = [jnp.concatenate([hi[side], jnp.zeros((96, 128), F32)], 0).T[0:64] for side in range(2)]
-    in_row(0, x, pltpu.roll(edges[0], 121, 1), pltpu.roll(edges[1], 120, 1))
+    for t in (0, 1, 2, 15, 16, 17):
+        x = (in_v[t - 1] if 0 < t < 17 else row_r[t // 17, 192:256, :]).astype(F32)
+        in_row(t, x, pltpu.roll(edges[0], 121 - t, 1), pltpu.roll(edges[1], 120 - t, 1))
+    beside = [
+        jnp.where(lane < 32, edges[0], in_edge[0]),
+        in_edge[1],
+        jnp.where(lane < 32, in_edge[2], pltpu.roll(edges[1], 32, 1)),
+    ]
+    beside = jnp.concatenate(
+        [(pltpu.roll(x, (1 - a) % 128, 1) if a != 1 else x).astype(BF16) for a in range(3) for x in beside], 0
+    )
     here = jnp.concatenate([in3[:, 0:128], in3[:, 128:256], in3[:, 256:384]], 0)
     fold = jnp.where(is_pole, in3[:, 128:256].astype(F32), 0.0).astype(BF16)
     there = jnp.concatenate([fold, jnp.zeros((384, 128), BF16)], 0)
@@ -527,6 +525,12 @@
 
     p1_start(1)
     p2_start(0)
+
+    for t in range(2, 16):
+        for i, (first, at_row) in enumerate(((0, 0), (112, 15), (128, 0), (144, 15))):
+            more = jnp.where(sub == at_row, jnp.broadcast_to(wide[t, i : i + 1, :], (16, 128)), 0.0)
+            cells = slice(first, first + 16)
+            g_v[t, cells, :] = ((ga_f[t, cells, :] + more) * slope_f[t, cells, :]).astype(BF16)
 
     def input_row(r):
         lhs = jnp.concatenate([g_v[r + 2], g_v[r + 1], g_v[r]], 1)
@@ -537,18 +541,19 @@
         t2 = pltpu.roll(t2, 1, 0)[0:128].T
         gi_o[r] = (t01[0:64] + t01[64:128] + t2).astype(BF16)
 
+    p2_start(1)
+
     @pl.loop(0, ROWS // 2, unroll=4)
     def _(r):
         input_row(r)
 
-    p2_start(1)
+    z_start(0)
+    z_start(1)
 
     @pl.loop(ROWS // 2, ROWS, unroll=4)
     def _(r):
         input_row(r)
 
-    z_start(0)
-    z_start(1)
     p4_start(0)
     p4_start(1)
     p5_start(0)
@@ -627,6 +632,7 @@
             vmem((192, 18 * 128), BF16),
             vmem((3, C0, 128), F32),
             vmem((128, 128), F32),
+            vmem((18, 8, 128), F32),
             vmem((18, WIDE, 128), BF16),
             vmem((18, WIDE, 128), F32),
             vmem((384, 384), F32),

time: 38.1 us -> 37.9 us (level)
  no operation moved by 1% of the time
where the time goes in v6:
time: 37.9 us; the launch traced here: 37.8 us
  Pallas kernels  37.1 us (98%)
  between operations  0.64 us (2%)
    pallas_call x1, Pallas kernels, section(): pl.pallas_call(functools.partial(kernel, nlat, nlon), out_shape=(vmem((RO...  36.1 us
    pallas_call x1, Pallas kernels, section(): pl.pallas_call(write_out, out_shape=(jax.ShapeDtypeStruct((ROWS, C0, COLS...  1.03 us

profile of v6, /device:TPU:1, one launch (start us, length us, event | category | flops | bytes accessed | tf_op | source)
XLA Modules:
  0.0 37.8 jit_solution(9080469858707425735)
XLA Ops:
  0.6 36.1 %shard_map.76 = (bf16[16,64,128]{2,1,0:T(8,128)(2,1)S(1)}, f32[2048,128]{1,0:T(8,128)S(1)}) custom-call(bf16[16,128,128]{2,1,0:T(8,128)(2,1)} %pre_h.1, bf16[16,64,128]{2,1,0:T(8,128)(2,1)} %bitcast.9, bf16[8,64,128]{2,1,0:T(8,128)(2,1)} %go_h.1, bf16[9,64,128]{2,1,0:T(8,128)(2,1)} %bitcast.11, bf16[9,128,128]{2,1,0:T(8,128)(2,1)} %bitcast.7), custom_call_target="tpu_custom_call" | custom-call | flops 1800000000 | bytes 3000000 | tf_op jit(solution)/shard_map/pallas_call | solution.py:605
  36.8 1.0 %shard_map.77 = (bf16[16,64,128]{2,1,0:T(8,128)(2,1)}, f32[576,128]{1,0:T(8,128)}, f32[1152,128]{1,0:T(8,128)}) custom-call(bf16[16,64,128]{2,1,0:T(8,128)(2,1)S(1)} %get-tuple-element.8.gi_v, f32[2048,128]{1,0:T(8,128)S(1)} %get-tuple-element.9.gw_v), custom_call_target="tpu_custom_call" | custom-call | tf_op jit(solution)/shard_map/pallas_call | solution.py:670

commit v7 on v6

--- a/solution.py
+++ b/solution.py
@@ -634,7 +634,7 @@
             vmem((128, 128), F32),
             vmem((18, 8, 128), F32),
             vmem((18, WIDE, 128), BF16),
-            vmem((18, WIDE, 128), F32),
+            vmem((19, WIDE, 128), F32),
             vmem((384, 384), F32),
             vmem((2, 2 * HALF, 128), F32),
             vmem((2, HALF, 128), BF16),

time: 37.9 us -> 37.9 us (level)
  no operation moved by 1% of the time
where the time goes in v7:
time: 37.9 us; the launch traced here: 37.8 us
  Pallas kernels  37.1 us (98%)
  between operations  0.64 us (2%)
    pallas_call x1, Pallas kernels, section(): pl.pallas_call(functools.partial(kernel, nlat, nlon), out_shape=(vmem((RO...  36.1 us
    pallas_call x1, Pallas kernels, section(): pl.pallas_call(write_out, out_shape=(jax.ShapeDtypeStruct((ROWS, C0, COLS...  1.03 us

profile of v7, /device:TPU:1, one launch (start us, length us, event | category | flops | bytes accessed | tf_op | source)
XLA Modules:
  0.0 37.8 jit_solution(13833002016193898548)
XLA Ops:
  0.6 36.1 %shard_map.76 = (bf16[16,64,128]{2,1,0:T(8,128)(2,1)S(1)}, f32[2048,128]{1,0:T(8,128)S(1)}) custom-call(bf16[16,128,128]{2,1,0:T(8,128)(2,1)} %pre_h.1, bf16[16,64,128]{2,1,0:T(8,128)(2,1)} %bitcast.9, bf16[8,64,128]{2,1,0:T(8,128)(2,1)} %go_h.1, bf16[9,64,128]{2,1,0:T(8,128)(2,1)} %bitcast.11, bf16[9,128,128]{2,1,0:T(8,128)(2,1)} %bitcast.7), custom_call_target="tpu_custom_call" | custom-call | flops 1800000000 | bytes 3000000 | tf_op jit(solution)/shard_map/pallas_call | solution.py:605
  36.8 1.0 %shard_map.77 = (bf16[16,64,128]{2,1,0:T(8,128)(2,1)}, f32[576,128]{1,0:T(8,128)}, f32[1152,128]{1,0:T(8,128)}) custom-call(bf16[16,64,128]{2,1,0:T(8,128)(2,1)S(1)} %get-tuple-element.8.gi_v, f32[2048,128]{1,0:T(8,128)S(1)} %get-tuple-element.9.gw_v), custom_call_target="tpu_custom_call" | custom-call | tf_op jit(solution)/shard_map/pallas_call | solution.py:670
